TPU v7x, 32 devices: a whole 2x2x4 slice. The times are simulated.
32 devices in a mesh: blk: 8 (over z, y), uly: 4 (over x, core).
Axes of the slice: x: 2, y: 2, z: 4, core: 2. Of those that a mesh axis runs over, the one named last changes fastest.
Arguments:
- queries: bfloat16 [4, 1024, 10240], P('uly', 'blk'), may hold values from -6 to 6
- key_states: bfloat16 [4, 1024, 1024], P('uly', 'blk'), may hold values from -6 to 6
- value_states: bfloat16 [4, 1024, 1024], P('uly', 'blk'), may hold values from -6 to 6
- attention_out: bfloat16 [4, 1024, 10240], P('uly', 'blk'), may hold values from -1.5 to 1.5
- output_grad: bfloat16 [4, 1024, 10240], P('uly', 'blk'), may hold values from -24 to 24
- log_totals: float32 [4, 80, 1024], P('uly', None, 'blk'), as said below
- block_order: int32 [8], replicated, may hold values from 0 to 7, as said below
- query_gain: float32 [128], replicated, may hold values from 0.5 to 1.5
- key_gain: float32 [128], replicated, may hold values from 0.5 to 1.5
Outputs:
- query_grad: bfloat16 [4, 1024, 10240], P('uly', 'blk')
- key_grad: bfloat16 [4, 1024, 1024], P('uly', 'blk')
- value_grad: bfloat16 [4, 1024, 1024], P('uly', 'blk')
- query_gain_grad: float32 [128], replicated
- key_gain_grad: float32 [128], replicated
Inputs may be any that keep to these rules, and one draw needn't show every extreme that they name: `block_order`: a permutation; entry b is the place in each sequence of the 128 rows that index b of blk holds. `log_totals`: logarithms of positive softmax totals.
All inputs are finite; a program needn't handle non-finite values.
Results may differ from a plain program's by a relative error of at most 0.0017.
The roundings to bfloat16 on the way count: a program that leaves them out, or rounds other values in their place, can miss the bound.
Values may be sent and summed in bfloat16 or wider, within the bound.
A program may use at most 320 MiB of HBM per device.

v0:
```python
import jax
import jax.numpy as jnp
from jax import lax
from jax.sharding import PartitionSpec as P

HEADS = 80
KV_HEADS = 8
HEAD_DIM = 128
GROUP = 10


norm_eps = 1e-06


def passed_along(value, axis, steps):
    count = lax.axis_size(axis)
    pairs = [(source, (source + steps) % count) for source in range(count)]
    return lax.ppermute(value, axis, pairs)


def normed(states, heads, gain, rows):
    values = states.astype(jnp.float32).reshape(rows, heads, HEAD_DIM)
    inverse = lax.rsqrt(jnp.mean(values * values, axis=2, keepdims=True) + norm_eps)
    unit = values * inverse
    return (unit, inverse, (unit * gain).astype(jnp.bfloat16))


def norm_back(grad, unit, inverse, gain):
    scaled = grad * gain
    inner = jnp.mean(scaled * unit, axis=2, keepdims=True)
    return (inverse * (scaled - unit * inner)).astype(jnp.bfloat16)


def per_device(
    queries,
    key_states,
    value_states,
    attention_out,
    output_grad,
    log_totals,
    block_order,
    query_gain,
    key_gain,
):
    n_blk = lax.axis_size("blk")
    block_rows = queries.shape[1]
    score_scale = HEAD_DIM ** (-0.5)
    query_unit, query_inverse, query_low = normed(queries[0], HEADS, query_gain, block_rows)
    key_unit, key_inverse, key_low = normed(key_states[0], KV_HEADS, key_gain, block_rows)
    query_heads = query_low.reshape(block_rows, KV_HEADS, GROUP, HEAD_DIM)
    grad_heads = output_grad[0].reshape(block_rows, KV_HEADS, GROUP, HEAD_DIM)
    value_heads = value_states[0].reshape(block_rows, KV_HEADS, HEAD_DIM)
    row_inner = jnp.sum(
        output_grad[0].reshape(block_rows, HEADS, HEAD_DIM).astype(jnp.float32)
        * attention_out[0].reshape(block_rows, HEADS, HEAD_DIM).astype(jnp.float32),
        axis=2,
    )
    row_inner = row_inner.reshape(block_rows, KV_HEADS, GROUP).transpose(1, 2, 0)
    log_sums = log_totals[0].reshape(KV_HEADS, GROUP, block_rows)
    cycle_index = lax.axis_index("blk")
    blk_range = jnp.arange(n_blk, dtype=jnp.int32)
    row_range = jnp.arange(block_rows, dtype=jnp.int32)

    def place_scalar(holder):
        return jnp.sum(jnp.where(blk_range == holder, block_order, 0))

    query_places = place_scalar(cycle_index) * block_rows + row_range

    def grads_for(key_piece, value_piece, key_places):

        def compute(key_part, value_part, places_part):
            scores = (
                jnp.einsum(
                    "qgph,kgh->gpqk", query_heads, key_part, preferred_element_type=jnp.float32
                )
                * score_scale
            )
            visible = places_part[None, :] <= query_places[:, None]
            probs = jnp.where(
                visible, jnp.exp(scores - log_sums[..., None]), jnp.zeros_like(scores)
            )
            dprobs = jnp.einsum(
                "qgph,kgh->gpqk", grad_heads, value_part, preferred_element_type=jnp.float32
            )
            dscores = (probs * (dprobs - row_inner[..., None])).astype(jnp.bfloat16)
            probs_low = probs.astype(jnp.bfloat16)
            query_add = jnp.einsum(
                "gpqk,kgh->qgph", dscores, key_part, preferred_element_type=jnp.float32
            )
            key_add = jnp.einsum(
                "gpqk,qgph->kgh", dscores, query_heads, preferred_element_type=jnp.float32
            )
            value_add = jnp.einsum(
                "gpqk,qgph->kgh", probs_low, grad_heads, preferred_element_type=jnp.float32
            )
            return (query_add, key_add, value_add)

        def skipped(key_part, value_part, places_part):
            piece_rows = key_part.shape[0]
            return (
                jnp.zeros((block_rows, KV_HEADS, GROUP, HEAD_DIM), jnp.float32),
                jnp.zeros((piece_rows, KV_HEADS, HEAD_DIM), jnp.float32),
                jnp.zeros((piece_rows, KV_HEADS, HEAD_DIM), jnp.float32),
            )

        needed = jnp.min(key_places) <= query_places[-1]
        return lax.cond(needed, compute, skipped, key_piece, value_piece, key_places)

    query_acc = jnp.zeros((block_rows, KV_HEADS, GROUP, HEAD_DIM), jnp.float32)
    empty_acc = jnp.zeros((block_rows, KV_HEADS, HEAD_DIM), jnp.float32)

    def send_grads(grad_pair):
        return passed_along((grad_pair[0], grad_pair[1]), "blk", 1)

    def absorb(rotation, keys_now, values_now, key_acc, value_acc, query_sum):
        holder = jnp.mod(cycle_index - rotation, n_blk)
        key_places = place_scalar(holder) * block_rows + row_range
        query_add, key_add, value_add = grads_for(keys_now, values_now, key_places)
        return (key_acc + key_add, value_acc + value_add, query_sum + query_add)

    def turn(rotation, carry_state):
        keys_now, values_now, key_acc, value_acc, query_sum = carry_state
        key_acc, value_acc, query_sum = absorb(
            rotation, keys_now, values_now, key_acc, value_acc, query_sum
        )
        keys_now, values_now = passed_along((keys_now, values_now), "blk", 1)
        key_acc, value_acc = send_grads((key_acc, value_acc))
        return (keys_now, values_now, key_acc, value_acc, query_sum)

    keys_now, values_now, key_acc, value_acc, query_acc = lax.fori_loop(
        0, n_blk - 1, turn, (key_low, value_heads, empty_acc, empty_acc, query_acc)
    )
    key_acc, value_acc, query_acc = absorb(
        n_blk - 1, keys_now, values_now, key_acc, value_acc, query_acc
    )
    key_acc, value_acc = send_grads((key_acc, value_acc))
    query_normed_grad = (query_acc * score_scale).reshape(block_rows, HEADS, HEAD_DIM)
    key_normed_grad = key_acc * score_scale
    query_term = jnp.sum(query_normed_grad * query_unit, axis=(0, 1))
    key_term = jnp.sum(key_normed_grad * key_unit, axis=(0, 1))
    query_gain_grad, key_gain_grad = lax.psum((query_term, key_term), ("blk", "uly"))
    query_grad = norm_back(query_normed_grad, query_unit, query_inverse, query_gain).reshape(
        1, block_rows, HEADS * HEAD_DIM
    )
    key_grad = norm_back(key_normed_grad, key_unit, key_inverse, key_gain).reshape(
        1, block_rows, KV_HEADS * HEAD_DIM
    )
    value_grad = value_acc.reshape(1, block_rows, KV_HEADS * HEAD_DIM).astype(jnp.bfloat16)
    return (query_grad, key_grad, value_grad, query_gain_grad, key_gain_grad)


def solution(mesh):
    return jax.shard_map(
        per_device,
        mesh=mesh,
        in_specs=(
            P("uly", "blk", None),
            P("uly", "blk", None),
            P("uly", "blk", None),
            P("uly", "blk", None),
            P("uly", "blk", None),
            P("uly", None, "blk"),
            P(),
            P(),
            P(),
        ),
        out_specs=(P("uly", "blk", None), P("uly", "blk", None), P("uly", "blk", None), P(), P()),
        check_vma=False,
    )
```

profile of v0, /device:TPU:0, one launch (start us, length us, event | category | flops | bytes accessed | tf_op | source)
XLA Modules:
  0.0 487.2 jit_solution(1027066436884426817)
XLA Ops:
  51.2 335.8 %while.24 = (s32[]{:T(128)}, bf16[128,8,128]{2,0,1:T(8,128)(2,1)S(1)}, bf16[128,8,128]{2,0,1:T(8,128)(2,1)}, f32[128,8,128]{2,0,1:T(8,128)}, f32[128,8,128]{2,0,...) while((s32[]{:T(128)}, ...), condition=%wide.region_9.10_spmd.clone, body=%wide.region_4.9_spmd.clone.sunk | while | flops 1693729024 | bytes 80210248 | solution.py:130
  62.8 13.4 %conditional.5 = (f32[128,8,10,128]{3,0,2,1:T(8,128)}, f32[128,8,128]{2,0,1:T(8,128)}, f32[128,8,128]{2,0,1:T(8,128)S(1)}) conditional(s32[]{:T(128)} %convert_element_type.134, () %tuple.85, (s32[128]{0:T(128)S(1)}, s32[128]{0:T(128)}, bf16[128,8,128]{2,0,1:T(8,128)(2,1)}, bf16[128,8,10,128]{3,0,2,1:T(8,128)(2,1)S(1)}, f32[1,80,128]{2,1,0:T(8,128)}, ...), branch_computations={%region_7.7_spmd, %region_8.8_spmd} | conditional | flops 1690845184 | bytes 51897396 | solution.py:107
  95.8 9.6 %collective-permute-done.2 = f32[128,8,128]{2,0,1:T(8,128)} collective-permute-done((f32[128,8,128]{2,0,1:T(8,128)}, f32[128,8,128]{2,0,1:T(8,128)}, u32[]{:S(2)}, u32[]{:S(2)}) %collective-permute-start.2) | collective-permute-done | bytes 524320 | tf_op jit(solution)/shard_map/while/body/eval_jaxpr/ppermute | solution.py:18
  113.8 13.4 %conditional.5 = (f32[128,8,10,128]{3,0,2,1:T(8,128)}, f32[128,8,128]{2,0,1:T(8,128)}, f32[128,8,128]{2,0,1:T(8,128)S(1)}) conditional(s32[]{:T(128)} %convert_element_type.134, () %tuple.85, (s32[128]{0:T(128)S(1)}, s32[128]{0:T(128)}, bf16[128,8,128]{2,0,1:T(8,128)(2,1)}, bf16[128,8,10,128]{3,0,2,1:T(8,128)(2,1)S(1)}, f32[1,80,128]{2,1,0:T(8,128)}, ...), branch_computations={%region_7.7_spmd, %region_8.8_spmd} | conditional | flops 1690845184 | bytes 51897396 | solution.py:107
  134.2 8.0 %select_add_fusion.2 = f32[128,8,10,128]{3,0,2,1:T(8,128)} fusion(f32[128,8,10,128]{3,0,2,1:T(8,128)} %get-tuple-element.656, f32[128,8,10,128]{3,0,2,1:T(8,128)} %get-tuple-element.686, pred[]{:T(512)S(6)} %compare.5), kind=kLoop, calls=%fused_computation.46.clone.1 | loop fusion | flops 2621440 | bytes 15728641 | tf_op jit(solution)/shard_map/while/body/eval_jaxpr/add | solution.py:119
  146.8 8.1 %collective-permute-done.2 = f32[128,8,128]{2,0,1:T(8,128)} collective-permute-done((f32[128,8,128]{2,0,1:T(8,128)}, f32[128,8,128]{2,0,1:T(8,128)}, u32[]{:S(2)}, u32[]{:S(2)}) %collective-permute-start.2) | collective-permute-done | bytes 524320 | tf_op jit(solution)/shard_map/while/body/eval_jaxpr/ppermute | solution.py:18
  163.3 13.3 %conditional.5 = (f32[128,8,10,128]{3,0,2,1:T(8,128)}, f32[128,8,128]{2,0,1:T(8,128)}, f32[128,8,128]{2,0,1:T(8,128)S(1)}) conditional(s32[]{:T(128)} %convert_element_type.134, () %tuple.85, (s32[128]{0:T(128)S(1)}, s32[128]{0:T(128)}, bf16[128,8,128]{2,0,1:T(8,128)(2,1)}, bf16[128,8,10,128]{3,0,2,1:T(8,128)(2,1)S(1)}, f32[1,80,128]{2,1,0:T(8,128)}, ...), branch_computations={%region_7.7_spmd, %region_8.8_spmd} | conditional | flops 1690845184 | bytes 51897396 | solution.py:107
  180.6 8.0 %select_add_fusion.2 = f32[128,8,10,128]{3,0,2,1:T(8,128)} fusion(f32[128,8,10,128]{3,0,2,1:T(8,128)} %get-tuple-element.656, f32[128,8,10,128]{3,0,2,1:T(8,128)} %get-tuple-element.686, pred[]{:T(512)S(6)} %compare.5), kind=kLoop, calls=%fused_computation.46.clone.1 | loop fusion | flops 2621440 | bytes 15728641 | tf_op jit(solution)/shard_map/while/body/eval_jaxpr/add | solution.py:119
  188.6 7.7 %collective-permute-done.3 = f32[128,8,128]{2,0,1:T(8,128)S(1)} collective-permute-done((f32[128,8,128]{2,0,1:T(8,128)}, f32[128,8,128]{2,0,1:T(8,128)S(1)}, u32[]{:S(2)}, u32[]{:S(2)}) %collective-permute-start.3) | collective-permute-done | bytes 524320 | tf_op jit(solution)/shard_map/while/body/eval_jaxpr/ppermute | solution.py:18
  196.3 6.6 %collective-permute-done.2 = f32[128,8,128]{2,0,1:T(8,128)} collective-permute-done((f32[128,8,128]{2,0,1:T(8,128)}, f32[128,8,128]{2,0,1:T(8,128)}, u32[]{:S(2)}, u32[]{:S(2)}) %collective-permute-start.2) | collective-permute-done | bytes 524320 | tf_op jit(solution)/shard_map/while/body/eval_jaxpr/ppermute | solution.py:18
  218.0 9.4 %collective-permute-start.2 = (f32[128,8,128]{2,0,1:T(8,128)}, f32[128,8,128]{2,0,1:T(8,128)}, u32[]{:S(2)}, u32[]{:S(2)}) collective-permute-start(f32[128,8,128]{2,0,1:T(8,128)} %add.187), channel_id=1, source_target_pairs={{0,4},{4,8},{8,12},{12,16},{16,20},{20,24},{24,28},{28,0},{1,5},{5... | collective-permute-start | bytes 1572872 | tf_op jit(solution)/shard_map/while/body/eval_jaxpr/ppermute | solution.py:18
  227.4 8.0 %select_add_fusion.2 = f32[128,8,10,128]{3,0,2,1:T(8,128)} fusion(f32[128,8,10,128]{3,0,2,1:T(8,128)} %get-tuple-element.656, f32[128,8,10,128]{3,0,2,1:T(8,128)} %get-tuple-element.686, pred[]{:T(512)S(6)} %compare.5), kind=kLoop, calls=%fused_computation.46.clone.1 | loop fusion | flops 2621440 | bytes 15728641 | tf_op jit(solution)/shard_map/while/body/eval_jaxpr/add | solution.py:119
  235.4 7.6 %collective-permute-done.3 = f32[128,8,128]{2,0,1:T(8,128)S(1)} collective-permute-done((f32[128,8,128]{2,0,1:T(8,128)}, f32[128,8,128]{2,0,1:T(8,128)S(1)}, u32[]{:S(2)}, u32[]{:S(2)}) %collective-permute-start.3) | collective-permute-done | bytes 524320 | tf_op jit(solution)/shard_map/while/body/eval_jaxpr/ppermute | solution.py:18
  255.9 13.3 %conditional.5 = (f32[128,8,10,128]{3,0,2,1:T(8,128)}, f32[128,8,128]{2,0,1:T(8,128)}, f32[128,8,128]{2,0,1:T(8,128)S(1)}) conditional(s32[]{:T(128)} %convert_element_type.134, () %tuple.85, (s32[128]{0:T(128)S(1)}, s32[128]{0:T(128)}, bf16[128,8,128]{2,0,1:T(8,128)(2,1)}, bf16[128,8,10,128]{3,0,2,1:T(8,128)(2,1)S(1)}, f32[1,80,128]{2,1,0:T(8,128)}, ...), branch_computations={%region_7.7_spmd, %region_8.8_spmd} | conditional | flops 1690845184 | bytes 51897396 | solution.py:107
  273.2 7.0 %collective-permute-start.2 = (f32[128,8,128]{2,0,1:T(8,128)}, f32[128,8,128]{2,0,1:T(8,128)}, u32[]{:S(2)}, u32[]{:S(2)}) collective-permute-start(f32[128,8,128]{2,0,1:T(8,128)} %add.187), channel_id=1, source_target_pairs={{0,4},{4,8},{8,12},{12,16},{16,20},{20,24},{24,28},{28,0},{1,5},{5... | collective-permute-start | bytes 1572872 | tf_op jit(solution)/shard_map/while/body/eval_jaxpr/ppermute | solution.py:18
  280.3 8.0 %select_add_fusion.2 = f32[128,8,10,128]{3,0,2,1:T(8,128)} fusion(f32[128,8,10,128]{3,0,2,1:T(8,128)} %get-tuple-element.656, f32[128,8,10,128]{3,0,2,1:T(8,128)} %get-tuple-element.686, pred[]{:T(512)S(6)} %compare.5), kind=kLoop, calls=%fused_computation.46.clone.1 | loop fusion | flops 2621440 | bytes 15728641 | tf_op jit(solution)/shard_map/while/body/eval_jaxpr/add | solution.py:119
  308.1 13.3 %conditional.5 = (f32[128,8,10,128]{3,0,2,1:T(8,128)}, f32[128,8,128]{2,0,1:T(8,128)}, f32[128,8,128]{2,0,1:T(8,128)S(1)}) conditional(s32[]{:T(128)} %convert_element_type.134, () %tuple.85, (s32[128]{0:T(128)S(1)}, s32[128]{0:T(128)}, bf16[128,8,128]{2,0,1:T(8,128)(2,1)}, bf16[128,8,10,128]{3,0,2,1:T(8,128)(2,1)S(1)}, f32[1,80,128]{2,1,0:T(8,128)}, ...), branch_computations={%region_7.7_spmd, %region_8.8_spmd} | conditional | flops 1690845184 | bytes 51897396 | solution.py:107
  325.4 8.0 %select_add_fusion.2 = f32[128,8,10,128]{3,0,2,1:T(8,128)} fusion(f32[128,8,10,128]{3,0,2,1:T(8,128)} %get-tuple-element.656, f32[128,8,10,128]{3,0,2,1:T(8,128)} %get-tuple-element.686, pred[]{:T(512)S(6)} %compare.5), kind=kLoop, calls=%fused_computation.46.clone.1 | loop fusion | flops 2621440 | bytes 15728641 | tf_op jit(solution)/shard_map/while/body/eval_jaxpr/add | solution.py:119
  338.1 8.7 %collective-permute-done.2 = f32[128,8,128]{2,0,1:T(8,128)} collective-permute-done((f32[128,8,128]{2,0,1:T(8,128)}, f32[128,8,128]{2,0,1:T(8,128)}, u32[]{:S(2)}, u32[]{:S(2)}) %collective-permute-start.2) | collective-permute-done | bytes 524320 | tf_op jit(solution)/shard_map/while/body/eval_jaxpr/ppermute | solution.py:18
  353.9 13.3 %conditional.5 = (f32[128,8,10,128]{3,0,2,1:T(8,128)}, f32[128,8,128]{2,0,1:T(8,128)}, f32[128,8,128]{2,0,1:T(8,128)S(1)}) conditional(s32[]{:T(128)} %convert_element_type.134, () %tuple.85, (s32[128]{0:T(128)S(1)}, s32[128]{0:T(128)}, bf16[128,8,128]{2,0,1:T(8,128)(2,1)}, bf16[128,8,10,128]{3,0,2,1:T(8,128)(2,1)S(1)}, f32[1,80,128]{2,1,0:T(8,128)}, ...), branch_computations={%region_7.7_spmd, %region_8.8_spmd} | conditional | flops 1690845184 | bytes 51897396 | solution.py:107
  371.2 8.0 %select_add_fusion.2 = f32[128,8,10,128]{3,0,2,1:T(8,128)} fusion(f32[128,8,10,128]{3,0,2,1:T(8,128)} %get-tuple-element.656, f32[128,8,10,128]{3,0,2,1:T(8,128)} %get-tuple-element.686, pred[]{:T(512)S(6)} %compare.5), kind=kLoop, calls=%fused_computation.46.clone.1 | loop fusion | flops 2621440 | bytes 15728641 | tf_op jit(solution)/shard_map/while/body/eval_jaxpr/add | solution.py:119
  386.9 23.2 %conditional.2 = (f32[128,8,128]{2,0,1:T(8,128)}, f32[128,8,10,128]{0,3,2,1:T(8,128)}, f32[128,8,128]{0,2,1:T(8,128)}) conditional(s32[]{:T(128)} %convert_element_type.107, () %tuple.47, (s32[128]{0:T(128)}, s32[128]{0:T(128)}, bf16[128,8,128]{2,0,1:T(8,128)(2,1)S(1)}, bf16[128,8,10,128]{0,3,2,1:T(8,128)(2,1)}, f32[1,80,128]{2,1,0:T(8,128)}, ...), branch_computations={%region_12.13_spmd, %region_13.14_spmd} | conditional | flops 1690845184 | bytes 84403312 | solution.py:107
  421.0 11.1 %multiply_reduce_fusion = (f32[128]{0:T(128)}, f32[128,8,10]{0,2,1:T(8,128)S(1)}, f32[128,8,10,128]{0,3,2,1:T(8,128)}) fusion(f32[128,8,10,128]{0,3,2,1:T(8,128)} %get-tuple-element.563, f32[128,8,10]{0,2,1:T(8,128)S(1)} %copy-done.11, f32[128]{0:T(128)S(1)} %broadcast_multiply_fusion.4, f32[128,8,10,128]{0,3,2,1:T(8,128)} %copy.53, ...), kind=kLoop, calls=%fused_computation.56 | loop fusion | flops 10475392 | bytes 21054464 | tf_op jit(solution)/shard_map/reduce_sum | solution.py:139
  446.6 40.6 %all-reduce = (f32[128]{0:T(128)}, f32[128]{0:T(128)}) all-reduce(f32[128]{0:T(128)S(1)} %copy-done.19, f32[128]{0:T(128)S(1)} %get-tuple-element.529), channel_id=1, replica_groups=mesh['blk'=8,'uly'=4] {'blk','uly'}, use_global_device_ids=true, to_apply=%region_17.18 | all-reduce | flops 256 | bytes 2048 | tf_op jit(solution)/shard_map/psum | solution.py:141
  (280 shorter events, 308.3 us)
Async XLA Ops:
  51.9 37.7 %collective-permute-start = (bf16[128,8,128]{2,0,1:T(8,128)(2,1)}, bf16[128,8,128]{2,0,1:T(8,128)(2,1)S(1)}, u32[]{:S(2)}, u32[]{:S(2)}) collective-permute-start(bf16[128,8,128]{2,0,1:T(8,128)(2,1)} %copy.90), channel_id=1, source_target_pairs={{0,4},{4,8},{8,12},{12,16},{16,20},{20,24},{24,28},{28,0},{1,5},{5... | collective-permute-start | bytes 786440 | tf_op jit(solution)/shard_map/while/body/eval_jaxpr/ppermute | solution.py:18
  56.5 33.1 %collective-permute-start.1 = (bf16[128,8,128]{2,0,1:T(8,128)(2,1)}, bf16[128,8,128]{2,0,1:T(8,128)(2,1)}, u32[]{:S(2)}, u32[]{:S(2)}) collective-permute-start(bf16[128,8,128]{2,0,1:T(8,128)(2,1)} %copy.91), channel_id=1, source_target_pairs={{0,4},{4,8},{8,12},{12,16},{16,20},{20,24},{24,28},{28,0},{1,5},{5... | collective-permute-start | bytes 786440 | tf_op jit(solution)/shard_map/while/body/eval_jaxpr/ppermute | solution.py:18
  78.1 17.8 %collective-permute-start.3 = (f32[128,8,128]{2,0,1:T(8,128)}, f32[128,8,128]{2,0,1:T(8,128)S(1)}, u32[]{:S(2)}, u32[]{:S(2)}) collective-permute-start(f32[128,8,128]{2,0,1:T(8,128)} %add.188), channel_id=1, source_target_pairs={{0,4},{4,8},{8,12},{12,16},{16,20},{20,24},{24,28},{28,0},{1,5},{5... | collective-permute-start | bytes 1572872 | tf_op jit(solution)/shard_map/while/body/eval_jaxpr/ppermute | solution.py:18
  81.6 23.8 %collective-permute-start.2 = (f32[128,8,128]{2,0,1:T(8,128)}, f32[128,8,128]{2,0,1:T(8,128)}, u32[]{:S(2)}, u32[]{:S(2)}) collective-permute-start(f32[128,8,128]{2,0,1:T(8,128)} %add.187), channel_id=1, source_target_pairs={{0,4},{4,8},{8,12},{12,16},{16,20},{20,24},{24,28},{28,0},{1,5},{5... | collective-permute-start | bytes 1572872 | tf_op jit(solution)/shard_map/while/body/eval_jaxpr/ppermute | solution.py:18
  106.1 36.1 %collective-permute-start = (bf16[128,8,128]{2,0,1:T(8,128)(2,1)}, bf16[128,8,128]{2,0,1:T(8,128)(2,1)S(1)}, u32[]{:S(2)}, u32[]{:S(2)}) collective-permute-start(bf16[128,8,128]{2,0,1:T(8,128)(2,1)} %copy.90), channel_id=1, source_target_pairs={{0,4},{4,8},{8,12},{12,16},{16,20},{20,24},{24,28},{28,0},{1,5},{5... | collective-permute-start | bytes 786440 | tf_op jit(solution)/shard_map/while/body/eval_jaxpr/ppermute | solution.py:18
  107.8 34.4 %collective-permute-start.1 = (bf16[128,8,128]{2,0,1:T(8,128)(2,1)}, bf16[128,8,128]{2,0,1:T(8,128)(2,1)}, u32[]{:S(2)}, u32[]{:S(2)}) collective-permute-start(bf16[128,8,128]{2,0,1:T(8,128)(2,1)} %copy.91), channel_id=1, source_target_pairs={{0,4},{4,8},{8,12},{12,16},{16,20},{20,24},{24,28},{28,0},{1,5},{5... | collective-permute-start | bytes 786440 | tf_op jit(solution)/shard_map/while/body/eval_jaxpr/ppermute | solution.py:18
  131.1 23.8 %collective-permute-start.2 = (f32[128,8,128]{2,0,1:T(8,128)}, f32[128,8,128]{2,0,1:T(8,128)}, u32[]{:S(2)}, u32[]{:S(2)}) collective-permute-start(f32[128,8,128]{2,0,1:T(8,128)} %add.187), channel_id=1, source_target_pairs={{0,4},{4,8},{8,12},{12,16},{16,20},{20,24},{24,28},{28,0},{1,5},{5... | collective-permute-start | bytes 1572872 | tf_op jit(solution)/shard_map/while/body/eval_jaxpr/ppermute | solution.py:18
  155.6 33.0 %collective-permute-start = (bf16[128,8,128]{2,0,1:T(8,128)(2,1)}, bf16[128,8,128]{2,0,1:T(8,128)(2,1)S(1)}, u32[]{:S(2)}, u32[]{:S(2)}) collective-permute-start(bf16[128,8,128]{2,0,1:T(8,128)(2,1)} %copy.90), channel_id=1, source_target_pairs={{0,4},{4,8},{8,12},{12,16},{16,20},{20,24},{24,28},{28,0},{1,5},{5... | collective-permute-start | bytes 786440 | tf_op jit(solution)/shard_map/while/body/eval_jaxpr/ppermute | solution.py:18
  157.3 31.3 %collective-permute-start.1 = (bf16[128,8,128]{2,0,1:T(8,128)(2,1)}, bf16[128,8,128]{2,0,1:T(8,128)(2,1)}, u32[]{:S(2)}, u32[]{:S(2)}) collective-permute-start(bf16[128,8,128]{2,0,1:T(8,128)(2,1)} %copy.91), channel_id=1, source_target_pairs={{0,4},{4,8},{8,12},{12,16},{16,20},{20,24},{24,28},{28,0},{1,5},{5... | collective-permute-start | bytes 786440 | tf_op jit(solution)/shard_map/while/body/eval_jaxpr/ppermute | solution.py:18
  180.6 22.3 %collective-permute-start.2 = (f32[128,8,128]{2,0,1:T(8,128)}, f32[128,8,128]{2,0,1:T(8,128)}, u32[]{:S(2)}, u32[]{:S(2)}) collective-permute-start(f32[128,8,128]{2,0,1:T(8,128)} %add.187), channel_id=1, source_target_pairs={{0,4},{4,8},{8,12},{12,16},{16,20},{20,24},{24,28},{28,0},{1,5},{5... | collective-permute-start | bytes 1572872 | tf_op jit(solution)/shard_map/while/body/eval_jaxpr/ppermute | solution.py:18
  203.6 31.8 %collective-permute-start = (bf16[128,8,128]{2,0,1:T(8,128)(2,1)}, bf16[128,8,128]{2,0,1:T(8,128)(2,1)S(1)}, u32[]{:S(2)}, u32[]{:S(2)}) collective-permute-start(bf16[128,8,128]{2,0,1:T(8,128)(2,1)} %copy.90), channel_id=1, source_target_pairs={{0,4},{4,8},{8,12},{12,16},{16,20},{20,24},{24,28},{28,0},{1,5},{5... | collective-permute-start | bytes 786440 | tf_op jit(solution)/shard_map/while/body/eval_jaxpr/ppermute | solution.py:18
  205.3 30.1 %collective-permute-start.1 = (bf16[128,8,128]{2,0,1:T(8,128)(2,1)}, bf16[128,8,128]{2,0,1:T(8,128)(2,1)}, u32[]{:S(2)}, u32[]{:S(2)}) collective-permute-start(bf16[128,8,128]{2,0,1:T(8,128)(2,1)} %copy.91), channel_id=1, source_target_pairs={{0,4},{4,8},{8,12},{12,16},{16,20},{20,24},{24,28},{28,0},{1,5},{5... | collective-permute-start | bytes 786440 | tf_op jit(solution)/shard_map/while/body/eval_jaxpr/ppermute | solution.py:18
  215.9 27.1 %collective-permute-start.3 = (f32[128,8,128]{2,0,1:T(8,128)}, f32[128,8,128]{2,0,1:T(8,128)S(1)}, u32[]{:S(2)}, u32[]{:S(2)}) collective-permute-start(f32[128,8,128]{2,0,1:T(8,128)} %add.188), channel_id=1, source_target_pairs={{0,4},{4,8},{8,12},{12,16},{16,20},{20,24},{24,28},{28,0},{1,5},{5... | collective-permute-start | bytes 1572872 | tf_op jit(solution)/shard_map/while/body/eval_jaxpr/ppermute | solution.py:18
  218.0 30.8 %collective-permute-start.2 = (f32[128,8,128]{2,0,1:T(8,128)}, f32[128,8,128]{2,0,1:T(8,128)}, u32[]{:S(2)}, u32[]{:S(2)}) collective-permute-start(f32[128,8,128]{2,0,1:T(8,128)} %add.187), channel_id=1, source_target_pairs={{0,4},{4,8},{8,12},{12,16},{16,20},{20,24},{24,28},{28,0},{1,5},{5... | collective-permute-start | bytes 1572872 | tf_op jit(solution)/shard_map/while/body/eval_jaxpr/ppermute | solution.py:18
  249.5 38.8 %collective-permute-start = (bf16[128,8,128]{2,0,1:T(8,128)(2,1)}, bf16[128,8,128]{2,0,1:T(8,128)(2,1)S(1)}, u32[]{:S(2)}, u32[]{:S(2)}) collective-permute-start(bf16[128,8,128]{2,0,1:T(8,128)(2,1)} %copy.90), channel_id=1, source_target_pairs={{0,4},{4,8},{8,12},{12,16},{16,20},{20,24},{24,28},{28,0},{1,5},{5... | collective-permute-start | bytes 786440 | tf_op jit(solution)/shard_map/while/body/eval_jaxpr/ppermute | solution.py:18
  251.1 37.2 %collective-permute-start.1 = (bf16[128,8,128]{2,0,1:T(8,128)(2,1)}, bf16[128,8,128]{2,0,1:T(8,128)(2,1)}, u32[]{:S(2)}, u32[]{:S(2)}) collective-permute-start(bf16[128,8,128]{2,0,1:T(8,128)(2,1)} %copy.91), channel_id=1, source_target_pairs={{0,4},{4,8},{8,12},{12,16},{16,20},{20,24},{24,28},{28,0},{1,5},{5... | collective-permute-start | bytes 786440 | tf_op jit(solution)/shard_map/while/body/eval_jaxpr/ppermute | solution.py:18
  273.2 20.6 %collective-permute-start.2 = (f32[128,8,128]{2,0,1:T(8,128)}, f32[128,8,128]{2,0,1:T(8,128)}, u32[]{:S(2)}, u32[]{:S(2)}) collective-permute-start(f32[128,8,128]{2,0,1:T(8,128)} %add.187), channel_id=1, source_target_pairs={{0,4},{4,8},{8,12},{12,16},{16,20},{20,24},{24,28},{28,0},{1,5},{5... | collective-permute-start | bytes 1572872 | tf_op jit(solution)/shard_map/while/body/eval_jaxpr/ppermute | solution.py:18
  294.6 38.8 %collective-permute-start = (bf16[128,8,128]{2,0,1:T(8,128)(2,1)}, bf16[128,8,128]{2,0,1:T(8,128)(2,1)S(1)}, u32[]{:S(2)}, u32[]{:S(2)}) collective-permute-start(bf16[128,8,128]{2,0,1:T(8,128)(2,1)} %copy.90), channel_id=1, source_target_pairs={{0,4},{4,8},{8,12},{12,16},{16,20},{20,24},{24,28},{28,0},{1,5},{5... | collective-permute-start | bytes 786440 | tf_op jit(solution)/shard_map/while/body/eval_jaxpr/ppermute | solution.py:18
  299.9 33.5 %collective-permute-start.1 = (bf16[128,8,128]{2,0,1:T(8,128)(2,1)}, bf16[128,8,128]{2,0,1:T(8,128)(2,1)}, u32[]{:S(2)}, u32[]{:S(2)}) collective-permute-start(bf16[128,8,128]{2,0,1:T(8,128)(2,1)} %copy.91), channel_id=1, source_target_pairs={{0,4},{4,8},{8,12},{12,16},{16,20},{20,24},{24,28},{28,0},{1,5},{5... | collective-permute-start | bytes 786440 | tf_op jit(solution)/shard_map/while/body/eval_jaxpr/ppermute | solution.py:18
  325.4 21.4 %collective-permute-start.2 = (f32[128,8,128]{2,0,1:T(8,128)}, f32[128,8,128]{2,0,1:T(8,128)}, u32[]{:S(2)}, u32[]{:S(2)}) collective-permute-start(f32[128,8,128]{2,0,1:T(8,128)} %add.187), channel_id=1, source_target_pairs={{0,4},{4,8},{8,12},{12,16},{16,20},{20,24},{24,28},{28,0},{1,5},{5... | collective-permute-start | bytes 1572872 | tf_op jit(solution)/shard_map/while/body/eval_jaxpr/ppermute | solution.py:18
  347.4 31.8 %collective-permute-start = (bf16[128,8,128]{2,0,1:T(8,128)(2,1)}, bf16[128,8,128]{2,0,1:T(8,128)(2,1)S(1)}, u32[]{:S(2)}, u32[]{:S(2)}) collective-permute-start(bf16[128,8,128]{2,0,1:T(8,128)(2,1)} %copy.90), channel_id=1, source_target_pairs={{0,4},{4,8},{8,12},{12,16},{16,20},{20,24},{24,28},{28,0},{1,5},{5... | collective-permute-start | bytes 786440 | tf_op jit(solution)/shard_map/while/body/eval_jaxpr/ppermute | solution.py:18
  349.1 30.1 %collective-permute-start.1 = (bf16[128,8,128]{2,0,1:T(8,128)(2,1)}, bf16[128,8,128]{2,0,1:T(8,128)(2,1)}, u32[]{:S(2)}, u32[]{:S(2)}) collective-permute-start(bf16[128,8,128]{2,0,1:T(8,128)(2,1)} %copy.91), channel_id=1, source_target_pairs={{0,4},{4,8},{8,12},{12,16},{16,20},{20,24},{24,28},{28,0},{1,5},{5... | collective-permute-start | bytes 786440 | tf_op jit(solution)/shard_map/while/body/eval_jaxpr/ppermute | solution.py:18
  411.2 32.2 %collective-permute-start.5 = (bf16[128,8,128]{2,0,1:T(8,128)(2,1)S(1)}, bf16[128,8,128]{2,0,1:T(8,128)(2,1)}, u32[]{:S(2)}, u32[]{:S(2)}) collective-permute-start(bf16[128,8,128]{2,0,1:T(8,128)(2,1)S(1)} %add.145), channel_id=1, source_target_pairs={{0,4},{4,8},{8,12},{12,16},{16,20},{20,24},{24,28},{28,0},{1,5},{5... | collective-permute-start | bytes 786440 | tf_op jit(solution)/shard_map/ppermute | solution.py:18
  414.5 30.9 %collective-permute-start.4 = (f32[128,8,128]{0,2,1:T(8,128)}, f32[128,8,128]{0,2,1:T(8,128)S(1)}, u32[]{:S(2)}, u32[]{:S(2)}) collective-permute-start(f32[128,8,128]{0,2,1:T(8,128)} %add.144), channel_id=1, source_target_pairs={{0,4},{4,8},{8,12},{12,16},{16,20},{20,24},{24,28},{28,0},{1,5},{5... | collective-permute-start | bytes 1572872 | tf_op jit(solution)/shard_map/ppermute | solution.py:18
  (45 other events, 447.1 us)
where the time goes:
time: 487 us
  other arithmetic  141 us (29%)
  local copies, waits for them, and re-layouts  84.7 us (17%)
  matrix products  83.5 us (17%)
  waiting for transfers between devices  82.7 us (17%)
  blocking collectives  40.6 us (8%)
  starting transfers between devices  36.7 us (8%)
  loops' own time  14.7 us (3%)
    add x23, other arithmetic, absorb(): return (key_acc + key_add, value_acc + value_add, query_sum + query_add)  85.2 us
    ppermute x30, waiting for transfers between devices, passed_along(): return lax.ppermute(value, axis, pairs)  82.7 us
    psum x1, blocking collectives, per_device(): lax.psum((query_term, key_term), ('blk', 'uly'))  40.6 us
    ppermute x30, starting transfers between devices, passed_along(): return lax.ppermute(value, axis, pairs)  36.7 us
    dot_general x7, matrix products, compute(): jnp.einsum('gpqk,kgh->qgph', dscores, key_part, preferred_element_type=jn...  30.7 us
    unnamed x43, local copies, waits for them, and re-layouts  28.3 us
    dot_general x7, matrix products, compute(): jnp.einsum('qgph,kgh->gpqk', grad_heads, value_part, preferred_element_ty...  19.2 us
    while x42, local copies, waits for them, and re-layouts  16.7 us
  transfers between devices with their start and end apart: 30, of which 13 were waited for; matrix products, arithmetic and copies ran while one was open for 47% of the time, Pallas kernels for 0%

commit v1 on v0

v1 whole, which is shorter than its diff:
```python
import functools

import jax
import jax.numpy as jnp
from jax import lax
from jax.experimental import pallas as pl
from jax.experimental.pallas import tpu as pltpu
from jax.sharding import PartitionSpec as P

HEADS = 80
KV_HEADS = 8
HEAD_DIM = 128
GROUP = 10
SCALE = HEAD_DIM ** (-0.5)
LOG2E = 1.4426950408889634
PAIRS = GROUP // 2

norm_eps = 1e-06
NT = (((1,), (1,)), ((), ()))
NN = (((1,), (0,)), ((), ()))


def dot(a, b, dims):
    return lax.dot_general(a, b, dims, preferred_element_type=jnp.float32)


def norm_back(grad, unit, inverse, gain):
    scaled = grad * gain
    inner = jnp.mean(scaled * unit, axis=-1, keepdims=True)
    return (inverse * (scaled - unit * inner)).astype(jnp.bfloat16)


def unit_of(values):
    inverse = lax.rsqrt(jnp.mean(values * values, axis=-1, keepdims=True) + norm_eps)
    return values * inverse, inverse


def attend_kernel(
    n_blk, rows, chunk,
    q_ref, do_ref, ao_ref, k_ref, v_ref, lt_ref, bias_ref, gain_ref,
    dq_ref, dk_ref, dv_ref, term_ref,
    qs, dos, stats, kt,
):
    group = pl.program_id(0)
    gain = gain_ref[...]
    lane = lax.broadcasted_iota(jnp.int32, (rows, HEAD_DIM), 1)
    inner = jnp.zeros((rows, HEAD_DIM), jnp.float32)
    for h in range(GROUP):
        cols = slice(h * HEAD_DIM, (h + 1) * HEAD_DIM)
        unit, _ = unit_of(q_ref[:, cols].astype(jnp.float32))
        qs[h // 2, pl.ds((h % 2) * rows, rows), :] = (unit * gain).astype(jnp.bfloat16)
        grad = do_ref[:, cols]
        dos[h // 2, pl.ds((h % 2) * rows, rows), :] = grad
        one = jnp.sum(
            grad.astype(jnp.float32) * ao_ref[:, cols].astype(jnp.float32), axis=1, keepdims=True
        )
        inner = jnp.where(lane == h, one, inner)
    inner = inner.T
    for h in range(GROUP):
        half = pl.ds((h % 2) * rows, rows)
        stats[h // 2, 0:1, half] = inner[h : h + 1, :]
        stats[h // 2, 1:2, half] = lt_ref[0, h : h + 1, :] * LOG2E
    for c in range(n_blk * rows // HEAD_DIM):
        part = pl.ds(c * HEAD_DIM, HEAD_DIM)
        kt[:, part] = k_ref[part, :].astype(jnp.float32).T.astype(jnp.bfloat16)
    dk_ref[...] = jnp.zeros_like(dk_ref)
    dv_ref[...] = jnp.zeros_like(dv_ref)

    @pl.when(group == 0)
    def _():
        term_ref[...] = jnp.zeros_like(term_ref)

    for pair in range(PAIRS):
        query = qs[pair]
        grad = dos[pair]
        row_inner = stats[pair, 0:1, :]
        totals = stats[pair, 1:2, :]
        dq_t = jnp.zeros((HEAD_DIM, 2 * rows), jnp.float32)
        for c in range(n_blk * rows // chunk):
            part = pl.ds(c * chunk, chunk)
            bias = bias_ref[part, :]
            scores = dot(k_ref[part, :], query, NT)
            probs = jnp.exp2(
                scores * (SCALE * LOG2E) - totals + jnp.concatenate([bias, bias], axis=1)
            )
            dprobs = dot(v_ref[part, :], grad, NT)
            dscores = (probs * (dprobs - row_inner)).astype(jnp.bfloat16)
            dv_ref[part, :] += dot(probs.astype(jnp.bfloat16), grad, NN)
            dk_ref[part, :] += dot(dscores, query, NN)
            dq_t += dot(kt[:, part], dscores, NN)
        dq = dq_t.T * SCALE
        for h in range(2):
            cols = pl.ds((2 * pair + h) * HEAD_DIM, HEAD_DIM)
            one = dq[h * rows : (h + 1) * rows, :]
            unit, inverse = unit_of(q_ref[:, cols].astype(jnp.float32))
            term_ref[...] += jnp.sum(one * unit, axis=0, keepdims=True)
            dq_ref[:, cols] = norm_back(one, unit, inverse, gain)


def attend(q, do, ao, k, v, lt, bias, gain, n_blk, rows):
    wide = GROUP * HEAD_DIM
    total = n_blk * rows
    chunk = 2 * rows
    side = pl.BlockSpec((rows, wide), lambda g: (0, g))
    keys = pl.BlockSpec((total, HEAD_DIM), lambda g: (0, g))
    return pl.pallas_call(
        functools.partial(attend_kernel, n_blk, rows, chunk),
        grid=(KV_HEADS,),
        in_specs=[
            side, side, side, keys, keys,
            pl.BlockSpec((1, GROUP, rows), lambda g: (g, 0, 0)),
            pl.BlockSpec((total, rows), lambda g: (0, 0)),
            pl.BlockSpec((1, HEAD_DIM), lambda g: (0, 0)),
        ],
        out_specs=[side, keys, keys, pl.BlockSpec((1, HEAD_DIM), lambda g: (0, 0))],
        out_shape=[
            jax.ShapeDtypeStruct((rows, HEADS * HEAD_DIM), jnp.bfloat16),
            jax.ShapeDtypeStruct((total, KV_HEADS * HEAD_DIM), jnp.float32),
            jax.ShapeDtypeStruct((total, KV_HEADS * HEAD_DIM), jnp.float32),
            jax.ShapeDtypeStruct((1, HEAD_DIM), jnp.float32),
        ],
        scratch_shapes=[
            pltpu.VMEM((PAIRS, 2 * rows, HEAD_DIM), jnp.bfloat16),
            pltpu.VMEM((PAIRS, 2 * rows, HEAD_DIM), jnp.bfloat16),
            pltpu.VMEM((PAIRS, 2, 2 * rows), jnp.float32),
            pltpu.VMEM((HEAD_DIM, total), jnp.bfloat16),
        ],
        compiler_params=pltpu.CompilerParams(
            dimension_semantics=("arbitrary",), vmem_limit_bytes=48 * 1024 * 1024
        ),
        cost_estimate=pl.CostEstimate(
            flops=10 * HEADS * rows * total * HEAD_DIM,
            bytes_accessed=8 * rows * HEADS * HEAD_DIM + 12 * total * KV_HEADS * HEAD_DIM,
            transcendentals=HEADS * rows * total,
        ),
    )(q, do, ao, k, v, lt, bias, gain)


def per_device(
    queries,
    key_states,
    value_states,
    attention_out,
    output_grad,
    log_totals,
    block_order,
    query_gain,
    key_gain,
):
    n_blk = lax.axis_size("blk")
    rows = queries.shape[1]
    key_unit, key_inverse = unit_of(
        key_states[0].astype(jnp.float32).reshape(rows, KV_HEADS, HEAD_DIM)
    )
    key_low = (key_unit * key_gain).astype(jnp.bfloat16).reshape(rows, KV_HEADS * HEAD_DIM)
    k_all = lax.all_gather(key_low, "blk", axis=0, tiled=True)
    v_all = lax.all_gather(value_states[0], "blk", axis=0, tiled=True)
    me = lax.axis_index("blk")
    inside = jnp.arange(rows, dtype=jnp.int32)
    places = (block_order[:, None] * rows + inside[None, :]).reshape(-1)
    own = jnp.sum(jnp.where(jnp.arange(n_blk) == me, block_order, 0)) * rows + inside
    bias = jnp.where(places[:, None] <= own[None, :], 0.0, -jnp.inf).astype(jnp.float32)
    dq, dk, dv, term = attend(
        queries[0], output_grad[0], attention_out[0], k_all, v_all,
        log_totals[0].reshape(KV_HEADS, GROUP, rows), bias, query_gain[None, :], n_blk, rows,
    )
    dk = lax.psum_scatter(dk, "blk", scatter_dimension=0, tiled=True)
    dv = lax.psum_scatter(dv, "blk", scatter_dimension=0, tiled=True)
    key_normed_grad = (dk * SCALE).reshape(rows, KV_HEADS, HEAD_DIM)
    key_term = jnp.sum(key_normed_grad * key_unit, axis=(0, 1))
    query_gain_grad, key_gain_grad = lax.psum((term[0], key_term), ("blk", "uly"))
    key_grad = norm_back(key_normed_grad, key_unit, key_inverse, key_gain).reshape(
        1, rows, KV_HEADS * HEAD_DIM
    )
    return (dq[None], key_grad, dv.astype(jnp.bfloat16)[None], query_gain_grad, key_gain_grad)


def solution(mesh):
    return jax.shard_map(
        per_device,
        mesh=mesh,
        in_specs=(
            P("uly", "blk", None),
            P("uly", "blk", None),
            P("uly", "blk", None),
            P("uly", "blk", None),
            P("uly", "blk", None),
            P("uly", None, "blk"),
            P(),
            P(),
            P(),
        ),
        out_specs=(P("uly", "blk", None), P("uly", "blk", None), P("uly", "blk", None), P(), P()),
        check_vma=False,
    )
```

time: 487 us -> 353 us (0.72)
  waiting for transfers between devices: 82.7 us -> 235 us
  other arithmetic: 141 us -> 7.32 us
  matrix products: 83.5 us -> 0 us
  local copies, waits for them, and re-layouts: 84.7 us -> 4.66 us
  Pallas kernels: 0 us -> 48.2 us
  starting transfers between devices: 36.7 us -> 0.16 us
  loops' own time: 14.7 us -> 0 us
  between operations: 3.61 us -> 14.6 us
    reduce_scatter x0 -> x2, waiting for transfers between devices: none -> 134 us  [the longest x1 85.9 us: per_device(): dk = lax.psum_scatter(dk, 'blk', scatter_dimension=0, tiled=True)]
    all_gather x0 -> x2, waiting for transfers between devices: none -> 99.9 us  [the longest x1 50 us: per_device(): k_all = lax.all_gather(key_low, 'blk', axis=0, tiled=True)]
    add x32 -> x2, other arithmetic: 92 us -> 0.07 us  [the longest x1 0.07 us: per_device(): places = (block_order[:, None] * rows + inside[None, :]).reshape(-1)]
    dot_general x35 -> x0, matrix products: 83.5 us -> none  [the longest x7 30.7 us: compute(): jnp.einsum('gpqk,kgh->qgph', dscores, key_part, preferred_element_type=jn...]
    ppermute x30 -> x0, waiting for transfers between devices: 82.7 us -> none  [passed_along(): return lax.ppermute(value, axis, pairs)]
    pallas_call x0 -> x1, Pallas kernels: none -> 48.2 us  [attend(): pl.pallas_call(functools.partial(attend_kernel, n_blk, rows, chunk), grid...]
    ppermute x30 -> x0, starting transfers between devices: 36.7 us -> none  [passed_along(): return lax.ppermute(value, axis, pairs)]
    unnamed x43 -> x18, local copies, waits for them, and re-layouts: 28.3 us -> 3.44 us
  transfers between devices with their start and end apart: 30 -> 4, of which waited for: 13 -> 4; matrix products, arithmetic and copies ran while one was open for 47% -> 1% of each run, Pallas kernels for 0% -> 0%
where the time goes in v1:
time: 353 us
  waiting for transfers between devices  235 us (67%)
  Pallas kernels  48.2 us (14%)
  blocking collectives  42.3 us (12%)
  between operations  14.6 us (4%)
  other arithmetic  7.32 us (2%)
  local copies, waits for them, and re-layouts  4.66 us (1%)
    reduce_scatter x1, waiting for transfers between devices, per_device(): dk = lax.psum_scatter(dk, 'blk', scatter_dimension=0, tiled=True)  85.9 us
    all_gather x1, waiting for transfers between devices, per_device(): k_all = lax.all_gather(key_low, 'blk', axis=0, tiled=True)  50 us
    all_gather x1, waiting for transfers between devices, per_device(): v_all = lax.all_gather(value_states[0], 'blk', axis=0, tiled=True)  49.9 us
    reduce_scatter x1, waiting for transfers between devices, per_device(): dv = lax.psum_scatter(dv, 'blk', scatter_dimension=0, tiled=True)  48.5 us
    pallas_call x1, Pallas kernels, attend(): pl.pallas_call(functools.partial(attend_kernel, n_blk, rows, chunk), grid...  48.2 us
    psum x1, blocking collectives, per_device(): lax.psum((term[0], key_term), ('blk', 'uly'))  42.3 us
  transfers between devices with their start and end apart: 4, of which 4 were waited for; matrix products, arithmetic and copies ran while one was open for 1% of the time, Pallas kernels for 0%

profile of v1, /device:TPU:0, one launch (start us, length us, event | category | flops | bytes accessed | tf_op | source)
XLA Modules:
  0.0 352.7 jit_solution(2062384693180793564)
XLA Ops:
  7.3 1.0 convert_bitcast_fusion
  8.3 0.1 copy.14
  8.4 0.2 multiply_reduce_fusion.2
  8.6 0.7 broadcast_bitcast_fusion
  9.3 0.2 mul.98
  9.5 0.8 multiply_convert_fusion
  10.4 0.7 all-gather.6.cloned.1.call-update
  11.2 0.6 broadcast_multiply_fusion.1
  12.6 0.2 compare_select_fusion.bias_ref
  12.8 50.0 %all-gather.4.cloned.1.call-done.k_ref = bf16[1024,1024]{1,0:T(8,128)(2,1)} async-done(((bf16[128,1024]{1,0:T(8,128)(2,1)}), bf16[1024,1024]{1,0:T(8,128)(2,1)}) %all-gather.4.cloned.1.call-update) | async-done | bytes 2097168 | tf_op jit(solution)/shard_map/all_gather | solution.py:156
  62.8 49.9 %all-gather.6.cloned.1.call-done = bf16[1,1024,1024]{2,1,0:T(8,128)(2,1)} async-done(((bf16[1,128,1024]{2,1,0:T(8,128)(2,1)}), bf16[1,1024,1024]{2,1,0:T(8,128)(2,1)}) %all-gather.6.cloned.1.call-update) | async-done | bytes 2097168 | tf_op jit(solution)/shard_map/all_gather | solution.py:157
  112.7 1.6 copy-done
  114.3 1.6 copy-done.1
  115.9 48.2 %shard_map.128 = (bf16[128,10240]{1,0:T(8,128)(2,1)}, f32[1024,1024]{1,0:T(8,128)}, f32[1024,1024]{1,0:T(8,128)}, f32[1,128]{1,0:T(1,128)S(1)}) custom-call(bf16[128,10240]{1,0:T(8,128)(2,1)} %bitcast.48, bf16[128,10240]{1,0:T(8,128)(2,1)} %bitcast.49, bf16[128,10240]{1,0:T(8,128)(2,1)} %bitcast.50, bf16[1024,1024]{1,0:T(8,128)(2,1)S(1)} %copy-done, ...), custom_call_target="tpu_custom_call" | custom-call | flops 13421772800 | bytes 23068672 | tf_op jit(solution)/shard_map/pallas_call | solution.py:106
  164.2 0.5 reduce-scatter.5.cloned.1.call-update
  164.8 85.9 %reduce-scatter.3.cloned.1.call-done = f32[128,1024]{1,0:T(8,128)} async-done(((f32[1024,1024]{1,0:T(8,128)}), f32[128,1024]{1,0:T(8,128)}) %reduce-scatter.3.cloned.1.call-update) | async-done | bytes 524304 | tf_op jit(solution)/shard_map/reduce_scatter | solution.py:167
  250.7 1.2 multiply_reduce_fusion
  251.9 0.1 copy.16
  252.1 0.4 multiply_reduce_fusion.1
  252.5 0.2 mul.120
  252.8 42.3 %all-reduce = (f32[128]{0:T(128)}, f32[128]{0:T(128)}) all-reduce(f32[128]{0:T(128)S(1)} %bitcast.43, f32[128]{0:T(128)S(1)} %bitcast_reduce_fusion), channel_id=1, replica_groups=mesh['blk'=8,'uly'=4] {'blk','uly'}, use_global_device_ids=true, to_apply=%region_5.6 | all-reduce | flops 256 | bytes 2048 | tf_op jit(solution)/shard_map/psum | solution.py:171
  295.0 48.5 %reduce-scatter.5.cloned.1.call-done = f32[128,1024]{1,0:T(8,128)} async-done(((f32[1024,1024]{1,0:T(8,128)}), f32[128,1024]{1,0:T(8,128)}) %reduce-scatter.5.cloned.1.call-update) | async-done | bytes 524304 | tf_op jit(solution)/shard_map/reduce_scatter | solution.py:168
  343.5 1.8 convert_bitcast_fusion.2
  345.3 0.9 fusion.4
  (30 shorter events, 0.6 us)
Async XLA Ops:
  7.2 2.3 copy-start.3
  7.2 4.0 %copy-start.5 = (f32[1,80,128]{2,1,0:T(8,128)S(1)}, f32[1,80,128]{2,1,0:T(8,128)}, u32[]{:S(2)}) copy-start(f32[1,80,128]{2,1,0:T(8,128)} %param.14) | copy-start | bytes 122884
  7.2 4.0 %copy-start.7 = (s32[8]{0:T(128)S(1)}, s32[8]{0:T(128)}, u32[]{:S(2)}) copy-start(s32[8]{0:T(128)} %param.15) | copy-start | bytes 100
  7.2 105.5 %copy-start.2 = (f32[128]{0:T(128)S(1)}, f32[128]{0:T(128)}, u32[]{:S(2)}) copy-start(f32[128]{0:T(128)} %param.16) | copy-start | bytes 1540
  7.2 55.6 %all-gather.4.cloned.1.call-start = ((), (), s32[]{:S(2)}) async-start(), calls=%async_computation.2 | async-start | bytes 2359296 | tf_op jit(solution)/shard_map/all_gather | solution.py:156
  10.4 102.3 %all-gather.6.cloned.1.call-start = ((), (), s32[]{:S(2)}) async-start(), calls=%async_computation.5 | async-start | bytes 2359296 | tf_op jit(solution)/shard_map/all_gather | solution.py:157
  11.1 239.6 %reduce-scatter.3.cloned.1.call-start = ((), (), s32[]{:S(2)}) async-start(), calls=%async_computation.3 | async-start | bytes 4718592 | tf_op jit(solution)/shard_map/reduce_scatter | solution.py:167
  112.7 1.6 copy-start
  114.3 1.6 copy-start.1
  164.1 179.4 %reduce-scatter.5.cloned.1.call-start = ((), (), s32[]{:S(2)}) async-start(), calls=%async_computation.4 | async-start | bytes 4718592 | tf_op jit(solution)/shard_map/reduce_scatter | solution.py:168
  164.2 0.7 copy-start.6
  252.0 93.3 %copy-start.4 = (f32[128,1024]{1,0:T(8,128)S(1)}, f32[128,1024]{1,0:T(8,128)}, u32[]{:S(2)}) copy-start(f32[128,1024]{1,0:T(8,128)} %reduce-scatter.3.cloned.1.call-done) | copy-start | bytes 1572868
Sparse Core Ops, SparseCore 0:
  10.7 51.9 all-gather.3
  64.9 47.7 all-gather.5
  164.2 86.4 reduce-scatter.2
  254.6 88.8 reduce-scatter.4

commit v2 on v1

v2 whole, which is shorter than its diff:
```python
import functools

import jax
import jax.numpy as jnp
from jax import lax
from jax.experimental import pallas as pl
from jax.experimental.pallas import tpu as pltpu
from jax.sharding import PartitionSpec as P

HEADS = 80
KV_HEADS = 8
HEAD_DIM = 128
GROUP = 10
SCALE = HEAD_DIM ** (-0.5)
LOG2E = 1.4426950408889634
PAIRS = GROUP // 2

norm_eps = 1e-06
NT = (((1,), (1,)), ((), ()))
NN = (((1,), (0,)), ((), ()))


def dot(a, b, dims):
    return lax.dot_general(a, b, dims, preferred_element_type=jnp.float32)


def norm_back(grad, unit, inverse, gain):
    scaled = grad * gain
    inner = jnp.mean(scaled * unit, axis=-1, keepdims=True)
    return (inverse * (scaled - unit * inner)).astype(jnp.bfloat16)


def unit_of(values):
    inverse = lax.rsqrt(jnp.mean(values * values, axis=-1, keepdims=True) + norm_eps)
    return values * inverse, inverse


STEPS = 32000.0
CODE_ROWS = 2 * HEAD_DIM + 16
MESH = pl.DeviceIdType.MESH


def code_half(x):
    most = jnp.maximum(jnp.max(jnp.abs(x), axis=0, keepdims=True), 1e-30)
    power = jnp.ceil(jnp.log2(most))
    return jnp.round(x * (STEPS * jnp.exp2(-power))).astype(jnp.int32).astype(jnp.int16), power


def encode(ref, index, keys, values, rows):
    code, key_power = code_half(keys)
    ref[(*index, pl.ds(0, rows), slice(None))] = code
    code, value_power = code_half(values)
    ref[(*index, pl.ds(rows, rows), slice(None))] = code
    row = lax.broadcasted_iota(jnp.int32, (16, HEAD_DIM), 0)
    powers = jnp.where(row == 0, key_power, value_power)
    ref[(*index, pl.ds(2 * rows, 16), slice(None))] = powers.astype(jnp.int32).astype(jnp.int16)


def as_f32(x):
    return x.astype(jnp.int32).astype(jnp.float32)


def decode(ref, index, rows):
    powers = as_f32(ref[(*index, pl.ds(2 * rows, 16), slice(None))])
    scale = jnp.exp2(powers) * (1.0 / STEPS)
    keys = as_f32(ref[(*index, pl.ds(0, rows), slice(None))]) * scale[0:1, :]
    values = as_f32(ref[(*index, pl.ds(rows, rows), slice(None))]) * scale[1:2, :]
    return keys, values


def fused_kernel(
    n_blk, n_uly, rows,
    q_ref, do_ref, ao_ref, key_ref, value_ref, lt_ref, bias_ref, gain_ref, key_gain_ref,
    dq_ref, dk_ref, dv_ref, q_term_ref, k_term_ref,
    qs, dos, stats, kt, kv, acc, y_out, y_in, z_out, z_in, own_sum, terms, blk_terms, uly_terms,
    kv_send, kv_recv, y_send, y_recv, z_send, z_recv, t_send, t_recv, u_send, u_recv,
):
    n_a = n_blk // 2
    step = pl.program_id(0)
    last = KV_HEADS - 1
    me = lax.axis_index("blk")
    uly = lax.axis_index("uly")
    a = me // 2
    b = me % 2
    partner = me + 1 - 2 * b
    gain = gain_ref[...]
    key_gain = key_gain_ref[...]

    def ring(d):
        return lax.rem(a + d, n_a)

    def kv_copy(g, block, slot, to):
        return pltpu.make_async_remote_copy(
            src_ref=kv.at[g, block], dst_ref=kv.at[g, block],
            send_sem=kv_send.at[g, slot], recv_sem=kv_recv.at[g, block],
            device_id=(to, uly), device_id_type=MESH,
        )

    def send_own(g):
        kv_copy(g, me, n_a - 1, partner).start()
        for d in range(1, n_a):
            kv_copy(g, me, d - 1, ring(d) * 2 + b).start()

    def forward(g):
        for d in range(1, n_a):
            block = ring(d) * 2 + b
            kv_copy(g, block, n_a - 1 + d, partner).wait_recv()
            kv_copy(g, block, n_a - 1 + d, partner).start()

    def gathered(g):
        for d in range(n_a):
            kv_copy(g, ring(d) * 2 + 1 - b, 0, partner).wait_recv()

    def y_copy(g):
        return pltpu.make_async_remote_copy(
            src_ref=y_out.at[g], dst_ref=y_in.at[g],
            send_sem=y_send.at[g], recv_sem=y_recv.at[g],
            device_id=(partner, uly), device_id_type=MESH,
        )

    def z_copy(g, d):
        return pltpu.make_async_remote_copy(
            src_ref=z_out.at[g, d - 1], dst_ref=z_in.at[g, d - 1],
            send_sem=z_send.at[g, d - 1], recv_sem=z_recv.at[g, d - 1],
            device_id=(ring(d) * 2 + b, uly), device_id_type=MESH,
        )

    def send_y(g):
        slot = lax.rem(g, 2)
        for i in range(n_a):
            part = acc.at[slot, i * 2 + 1 - b]
            encode(y_out, (g, i), part[0:rows, :], part[rows : 2 * rows, :], rows)
        y_copy(g).start()

    def send_z(g):
        slot = lax.rem(g, 2)
        y_copy(g).wait_recv()
        for d in range(n_a):
            i = ring(d)
            keys, values = decode(y_in, (g, i), rows)
            part = acc.at[slot, i * 2 + b]
            keys += part[0:rows, :]
            values += part[rows : 2 * rows, :]
            if d == 0:
                own_sum[g, 0:rows, :] = keys
                own_sum[g, rows : 2 * rows, :] = values
            else:
                encode(z_out, (g, d - 1), keys, values, rows)
                z_copy(g, d).start()

    def finish(g):
        keys = own_sum[g, 0:rows, :]
        values = own_sum[g, rows : 2 * rows, :]
        for d in range(1, n_a):
            z_copy(g, d).wait_recv()
            more_keys, more_values = decode(z_in, (g, d - 1), rows)
            keys += more_keys
            values += more_values
        cols = pl.ds(pl.multiple_of(g * HEAD_DIM, HEAD_DIM), HEAD_DIM)
        keys = keys * SCALE
        unit, inverse = unit_of(key_ref[:, cols].astype(jnp.float32))
        terms[1:2, :] += jnp.sum(keys * unit, axis=0, keepdims=True)
        dk_ref[:, cols] = norm_back(keys, unit, inverse, key_gain)
        dv_ref[:, cols] = values.astype(jnp.bfloat16)

    @pl.when(step == 0)
    def _():
        barrier = pltpu.get_barrier_semaphore()
        for d in range(1, n_blk):
            pl.semaphore_signal(
                barrier, inc=1, device_id=(lax.rem(me + d, n_blk), uly), device_id_type=MESH
            )
        for d in range(1, n_uly):
            pl.semaphore_signal(
                barrier, inc=1, device_id=(me, lax.rem(uly + d, n_uly)), device_id_type=MESH
            )
        terms[...] = jnp.zeros_like(terms)
        for g in range(KV_HEADS):
            cols = slice(g * HEAD_DIM, (g + 1) * HEAD_DIM)
            unit, _ = unit_of(key_ref[:, cols].astype(jnp.float32))
            kv[g, me, 0:rows, :] = (unit * key_gain).astype(jnp.bfloat16)
            kv[g, me, rows : 2 * rows, :] = value_ref[:, cols]
        pl.semaphore_wait(barrier, n_blk + n_uly - 2)
        for g in range(AHEAD):
            send_own(g)
        for g in range(AHEAD - 1):
            forward(g)

    @pl.when(step + AHEAD <= last)
    def _():
        send_own(step + AHEAD)

    @pl.when(step + AHEAD - 1 <= last)
    def _():
        forward(step + AHEAD - 1)

    @pl.when(step >= 2)
    def _():
        finish(step - 2)

    lane = lax.broadcasted_iota(jnp.int32, (rows, HEAD_DIM), 1)
    inner = jnp.zeros((rows, HEAD_DIM), jnp.float32)
    for h in range(GROUP):
        cols = slice(h * HEAD_DIM, (h + 1) * HEAD_DIM)
        unit, _ = unit_of(q_ref[:, cols].astype(jnp.float32))
        qs[h // 2, pl.ds((h % 2) * rows, rows), :] = (unit * gain).astype(jnp.bfloat16)
        grad = do_ref[:, cols]
        dos[h // 2, pl.ds((h % 2) * rows, rows), :] = grad
        one = jnp.sum(
            grad.astype(jnp.float32) * ao_ref[:, cols].astype(jnp.float32), axis=1, keepdims=True
        )
        inner = jnp.where(lane == h, one, inner)
    inner = inner.T
    for h in range(GROUP):
        half = pl.ds((h % 2) * rows, rows)
        stats[h // 2, 0:1, half] = inner[h : h + 1, :]
        stats[h // 2, 1:2, half] = lt_ref[0, h : h + 1, :] * LOG2E

    gathered(step)
    slot = lax.rem(step, 2)
    for i in range(n_blk):
        kt[:, i * rows : (i + 1) * rows] = (
            kv[step, i, 0:rows, :].astype(jnp.float32).T.astype(jnp.bfloat16)
        )
    acc[slot] = jnp.zeros((n_blk, 2 * rows, HEAD_DIM), jnp.float32)

    def one_pair(pair, carry):
        query = qs[pair]
        grad = dos[pair]
        row_inner = stats[pair, 0:1, :]
        totals = stats[pair, 1:2, :]
        dq_t = jnp.zeros((HEAD_DIM, 2 * rows), jnp.float32)
        for c in range(n_a):
            both = pl.ds(2 * c, 2)
            part = pl.ds(c * 2 * rows, 2 * rows)
            keys = kv[step, both, 0:rows, :].reshape(2 * rows, HEAD_DIM)
            values = kv[step, both, rows : 2 * rows, :].reshape(2 * rows, HEAD_DIM)
            bias = bias_ref[part, :]
            scores = dot(keys, query, NT)
            probs = jnp.exp2(
                scores * (SCALE * LOG2E) - totals + jnp.concatenate([bias, bias], axis=1)
            )
            dprobs = dot(values, grad, NT)
            dscores = (probs * (dprobs - row_inner)).astype(jnp.bfloat16)
            acc[slot, both, rows : 2 * rows, :] += dot(
                probs.astype(jnp.bfloat16), grad, NN
            ).reshape(2, rows, HEAD_DIM)
            acc[slot, both, 0:rows, :] += dot(dscores, query, NN).reshape(2, rows, HEAD_DIM)
            dq_t += dot(kt[:, part], dscores, NN)
        dq = dq_t.T * SCALE
        for h in range(2):
            cols = pl.ds(pl.multiple_of((2 * pair + h) * HEAD_DIM, HEAD_DIM), HEAD_DIM)
            one = dq[h * rows : (h + 1) * rows, :]
            unit, inverse = unit_of(q_ref[:, cols].astype(jnp.float32))
            terms[0:1, :] += jnp.sum(one * unit, axis=0, keepdims=True)
            dq_ref[:, cols] = norm_back(one, unit, inverse, gain)
        return carry

    lax.fori_loop(0, PAIRS, one_pair, 0)
    send_y(step)

    @pl.when(step >= 1)
    def _():
        send_z(step - 1)

    @pl.when(step == last)
    def _():
        finish(last - 1)
        send_z(last)
        finish(last)

        def term_copy(ref, index, sends, recvs, d, to):
            return pltpu.make_async_remote_copy(
                src_ref=ref.at[index], dst_ref=ref.at[index],
                send_sem=sends.at[d - 1], recv_sem=recvs.at[index],
                device_id=to, device_id_type=MESH,
            )

        def share(ref, mine, count, sends, recvs, to):
            for d in range(1, count):
                term_copy(ref, mine, sends, recvs, d, to(d)).start()
            for d in range(1, count):
                term_copy(ref, lax.rem(mine + d, count), sends, recvs, d, to(d)).wait_recv()
            total = ref[0]
            for i in range(1, count):
                total = total + ref[i]
            return total

        blk_terms[me] = terms[...]
        uly_terms[uly] = share(
            blk_terms, me, n_blk, t_send, t_recv, lambda d: (lax.rem(me + d, n_blk), uly)
        )
        total = share(
            uly_terms, uly, n_uly, u_send, u_recv, lambda d: (me, lax.rem(uly + d, n_uly))
        )
        q_term_ref[...] = total[0:1, :]
        k_term_ref[...] = total[1:2, :]
        for d in range(1, n_blk):
            term_copy(blk_terms, me, t_send, t_recv, d, (lax.rem(me + d, n_blk), uly)).wait_send()
        for d in range(1, n_uly):
            term_copy(uly_terms, uly, u_send, u_recv, d, (me, lax.rem(uly + d, n_uly))).wait_send()

        def drain(g, carry):
            for slot in range(2 * n_a - 1):
                kv_copy(g, me, slot, partner).wait_send()
            y_copy(g).wait_send()
            for d in range(1, n_a):
                z_copy(g, d).wait_send()
            return carry

        lax.fori_loop(0, KV_HEADS, drain, 0)


AHEAD = 3


def fused(q, do, ao, keys, values, lt, bias, gain, key_gain, n_blk, n_uly, rows):
    wide = GROUP * HEAD_DIM
    total = n_blk * rows
    n_a = n_blk // 2
    dma = pltpu.SemaphoreType.DMA
    side = pl.BlockSpec((rows, wide), lambda g: (0, g))
    whole = pl.BlockSpec((rows, KV_HEADS * HEAD_DIM), lambda g: (0, 0))
    line = pl.BlockSpec((1, HEAD_DIM), lambda g: (0, 0))
    code = (CODE_ROWS, HEAD_DIM)
    return pl.pallas_call(
        functools.partial(fused_kernel, n_blk, n_uly, rows),
        grid=(KV_HEADS,),
        in_specs=[
            side, side, side, whole, whole,
            pl.BlockSpec((1, GROUP, rows), lambda g: (g, 0, 0)),
            pl.BlockSpec((total, rows), lambda g: (0, 0)),
            line, line,
        ],
        out_specs=[side, whole, whole, line, line],
        out_shape=[
            jax.ShapeDtypeStruct((rows, HEADS * HEAD_DIM), jnp.bfloat16),
            jax.ShapeDtypeStruct((rows, KV_HEADS * HEAD_DIM), jnp.bfloat16),
            jax.ShapeDtypeStruct((rows, KV_HEADS * HEAD_DIM), jnp.bfloat16),
            jax.ShapeDtypeStruct((1, HEAD_DIM), jnp.float32),
            jax.ShapeDtypeStruct((1, HEAD_DIM), jnp.float32),
        ],
        scratch_shapes=[
            pltpu.VMEM((PAIRS, 2 * rows, HEAD_DIM), jnp.bfloat16),
            pltpu.VMEM((PAIRS, 2 * rows, HEAD_DIM), jnp.bfloat16),
            pltpu.VMEM((PAIRS, 2, 2 * rows), jnp.float32),
            pltpu.VMEM((HEAD_DIM, total), jnp.bfloat16),
            pltpu.VMEM((KV_HEADS, n_blk, 2 * rows, HEAD_DIM), jnp.bfloat16),
            pltpu.VMEM((2, n_blk, 2 * rows, HEAD_DIM), jnp.float32),
            pltpu.VMEM((KV_HEADS, n_a, *code), jnp.int16),
            pltpu.VMEM((KV_HEADS, n_a, *code), jnp.int16),
            pltpu.VMEM((KV_HEADS, n_a - 1, *code), jnp.int16),
            pltpu.VMEM((KV_HEADS, n_a - 1, *code), jnp.int16),
            pltpu.VMEM((KV_HEADS, 2 * rows, HEAD_DIM), jnp.float32),
            pltpu.VMEM((8, HEAD_DIM), jnp.float32),
            pltpu.VMEM((n_blk, 8, HEAD_DIM), jnp.float32),
            pltpu.VMEM((n_uly, 8, HEAD_DIM), jnp.float32),
            dma((KV_HEADS, 2 * n_a - 1)),
            dma((KV_HEADS, n_blk)),
            dma((KV_HEADS,)),
            dma((KV_HEADS,)),
            dma((KV_HEADS, n_a - 1)),
            dma((KV_HEADS, n_a - 1)),
            dma((n_blk - 1,)),
            dma((n_blk,)),
            dma((n_uly - 1,)),
            dma((n_uly,)),
        ],
        compiler_params=pltpu.CompilerParams(
            dimension_semantics=("arbitrary",),
            vmem_limit_bytes=56 * 1024 * 1024,
            collective_id=0,
            has_side_effects=True,
        ),
        cost_estimate=pl.CostEstimate(
            flops=10 * HEADS * rows * total * HEAD_DIM,
            bytes_accessed=8 * rows * HEADS * HEAD_DIM,
            transcendentals=HEADS * rows * total,
        ),
    )(q, do, ao, keys, values, lt, bias, gain, key_gain)


def per_device(
    queries,
    key_states,
    value_states,
    attention_out,
    output_grad,
    log_totals,
    block_order,
    query_gain,
    key_gain,
):
    n_blk = lax.axis_size("blk")
    n_uly = lax.axis_size("uly")
    rows = queries.shape[1]
    me = lax.axis_index("blk")
    inside = jnp.arange(rows, dtype=jnp.int32)
    places = (block_order[:, None] * rows + inside[None, :]).reshape(-1)
    own = jnp.sum(jnp.where(jnp.arange(n_blk) == me, block_order, 0)) * rows + inside
    bias = jnp.where(places[:, None] <= own[None, :], 0.0, -jnp.inf).astype(jnp.float32)
    dq, dk, dv, query_term, key_term = fused(
        queries[0], output_grad[0], attention_out[0], key_states[0], value_states[0],
        log_totals[0].reshape(KV_HEADS, GROUP, rows), bias, query_gain[None, :],
        key_gain[None, :], n_blk, n_uly, rows,
    )
    return (dq[None], dk[None], dv[None], query_term[0], key_term[0])


def solution(mesh):
    return jax.shard_map(
        per_device,
        mesh=mesh,
        in_specs=(
            P("uly", "blk", None),
            P("uly", "blk", None),
            P("uly", "blk", None),
            P("uly", "blk", None),
            P("uly", "blk", None),
            P("uly", None, "blk"),
            P(),
            P(),
            P(),
        ),
        out_specs=(P("uly", "blk", None), P("uly", "blk", None), P("uly", "blk", None), P(), P()),
        check_vma=False,
    )
```

time: 353 us -> 159 us (0.45)
  waiting for transfers between devices: 235 us -> 0 us
  Pallas kernels: 48.2 us -> 148 us
  blocking collectives: 42.3 us -> 0 us
  between operations: 14.6 us -> 1.34 us
  other arithmetic: 7.32 us -> 2.36 us
    reduce_scatter x2 -> x0, waiting for transfers between devices: 134 us -> none  [the longest x1 85.9 us: per_device(): dk = lax.psum_scatter(dk, 'blk', scatter_dimension=0, tiled=True)]
    all_gather x2 -> x0, waiting for transfers between devices: 99.9 us -> none  [the longest x1 50 us: per_device(): k_all = lax.all_gather(key_low, 'blk', axis=0, tiled=True)]
    pallas_call x1, Pallas kernels: 48.2 us -> 148 us  [fused(): pl.pallas_call(functools.partial(fused_kernel, n_blk, n_uly, rows), grid=...]
    psum x1 -> x0, blocking collectives: 42.3 us -> none  [per_device(): lax.psum((term[0], key_term), ('blk', 'uly'))]
  transfers between devices with their start and end apart: 4 -> 0, of which waited for: 4 -> 0; matrix products, arithmetic and copies ran while one was open for 1% -> 0% of each run, Pallas kernels for 0% -> 0%
where the time goes in v2:
time: 159 us
  Pallas kernels  148 us (93%)
  local copies, waits for them, and re-layouts  7.37 us (5%)
  other arithmetic  2.36 us (1%)
    pallas_call x1, Pallas kernels, fused(): pl.pallas_call(functools.partial(fused_kernel, n_blk, n_uly, rows), grid=...  148 us
    unnamed x13, local copies, waits for them, and re-layouts  5.96 us

profile of v2, /device:TPU:0, one launch (start us, length us, event | category | flops | bytes accessed | tf_op | source)
XLA Modules:
  0.0 158.9 jit_solution(7238555453957918864)
XLA Ops:
  0.6 1.3 broadcast_multiply_fusion
  2.6 0.1 add_bitcast_fusion
  2.7 1.4 reshape_squeeze.3.lt_ref
  4.1 1.0 compare_select_fusion.bias_ref
  5.1 147.8 %shard_map.128 = (bf16[128,10240]{1,0:T(8,128)(2,1)}, bf16[128,1024]{1,0:T(8,128)(2,1)}, bf16[128,1024]{1,0:T(8,128)(2,1)}, f32[1,128]{1,0:T(1,128)}, f32[1,128]{1,0:T(1,128)}) custom-call(bf16[128,10240]{1,0:T(8,128)(2,1)} %bitcast.17, bf16[128,10240]{1,0:T(8,128)(2,1)} %bitcast.18, bf16[128,10240]{1,0:T(8,128)(2,1)} %bitcast.19, ...), custom_call_target="tpu_custom_call" | custom-call | flops 13421772800 | bytes 10485760 | tf_op jit(solution)/shard_map/pallas_call | solution.py:326
  152.9 0.0 copy-start.1
  152.9 0.0 copy-start
  152.9 0.0 copy-start.3
  152.9 0.0 copy-start.2
  152.9 3.5 %copy.19 = bf16[1,128,10240]{2,1,0:T(8,128)(2,1)} copy(bf16[1,128,10240]{2,1,0:T(8,128)(2,1)} %bitcast.14) | data formatting | bytes 5242880
  156.4 0.0 copy-done.1
  156.5 0.7 copy.20
  157.2 0.0 copy-done
  157.2 0.7 copy.21
  157.9 0.0 copy-done.3
  157.9 0.5 copy.22
  158.4 0.0 copy-done.2
  158.4 0.5 copy.23
  (1 shorter events, 0.0 us)
Async XLA Ops:
  152.9 3.6 %copy-start.1 = (bf16[128,1024]{1,0:T(8,128)(2,1)S(1)}, bf16[128,1024]{1,0:T(8,128)(2,1)}, u32[]{:S(2)}) copy-start(bf16[128,1024]{1,0:T(8,128)(2,1)} %get-tuple-element.11) | copy-start | bytes 786436
  152.9 4.3 %copy-start = (bf16[128,1024]{1,0:T(8,128)(2,1)S(1)}, bf16[128,1024]{1,0:T(8,128)(2,1)}, u32[]{:S(2)}) copy-start(bf16[128,1024]{1,0:T(8,128)(2,1)} %get-tuple-element.12) | copy-start | bytes 786436
  152.9 4.9 %copy-start.3 = (f32[1,128]{1,0:T(1,128)S(1)}, f32[1,128]{1,0:T(1,128)}, u32[]{:S(2)}) copy-start(f32[1,128]{1,0:T(1,128)} %get-tuple-element.13) | copy-start | bytes 1540
  152.9 5.5 %copy-start.2 = (f32[1,128]{1,0:T(1,128)S(1)}, f32[1,128]{1,0:T(1,128)}, u32[]{:S(2)}) copy-start(f32[1,128]{1,0:T(1,128)} %get-tuple-element.14) | copy-start | bytes 1540

commit v3 on v2

v3 whole, which is shorter than its diff:
```python
import functools

import jax
import jax.numpy as jnp
from jax import lax
from jax.experimental import pallas as pl
from jax.experimental.pallas import tpu as pltpu
from jax.sharding import PartitionSpec as P

HEADS = 80
KV_HEADS = 8
HEAD_DIM = 128
GROUP = 10
SCALE = HEAD_DIM ** (-0.5)
LOG2E = 1.4426950408889634
PAIRS = GROUP // 2

norm_eps = 1e-06
NT = (((1,), (1,)), ((), ()))
NN = (((1,), (0,)), ((), ()))


def dot(a, b, dims):
    return lax.dot_general(a, b, dims, preferred_element_type=jnp.float32)


def norm_back(grad, unit, inverse, gain):
    scaled = grad * gain
    inner = jnp.mean(scaled * unit, axis=-1, keepdims=True)
    return (inverse * (scaled - unit * inner)).astype(jnp.bfloat16)


def unit_of(values):
    inverse = lax.rsqrt(jnp.mean(values * values, axis=-1, keepdims=True) + norm_eps)
    return values * inverse, inverse


STEPS = 32000.0
CODE_ROWS = HEAD_DIM + 16
MESH = pl.DeviceIdType.MESH


def encode(ref, index, x, rows):
    most = jnp.maximum(jnp.max(jnp.abs(x), axis=0, keepdims=True), 1e-30)
    power = jnp.ceil(jnp.log2(most))
    code = jnp.round(x * (STEPS * jnp.exp2(-power))).astype(jnp.int32).astype(jnp.int16)
    ref[(*index, pl.ds(0, rows), slice(None))] = code
    powers = jnp.broadcast_to(power, (16, HEAD_DIM))
    ref[(*index, pl.ds(rows, 16), slice(None))] = powers.astype(jnp.int32).astype(jnp.int16)


def as_f32(x):
    return x.astype(jnp.int32).astype(jnp.float32)


def decode(ref, index, rows):
    powers = as_f32(ref[(*index, pl.ds(rows, 16), slice(None))])
    scale = jnp.exp2(powers[0:1, :]) * (1.0 / STEPS)
    return as_f32(ref[(*index, pl.ds(0, rows), slice(None))]) * scale


def fused_kernel(
    n_blk, n_uly, rows,
    q_ref, do_ref, ao_ref, key_ref, value_ref, lt_ref, bias_ref, gain_ref, key_gain_ref,
    dq_ref, dk_ref, dv_ref, q_term_ref, k_term_ref,
    qs, dos, stats, kt, kv, acc, y_out, y_in, line_out, line_in, v_out, v_in,
    terms, blk_terms, uly_terms,
    kv_send, kv_recv, y_send, y_recv, line_send, line_recv, v_send, v_recv,
    t_send, t_recv, u_send, u_recv,
):
    n_a = n_blk // 2
    now = pl.program_id(0)
    step = now - n_a
    last = KV_HEADS - 1
    me = lax.axis_index("blk")
    uly = lax.axis_index("uly")
    a = me // 2
    b = me % 2
    other = 1 - b
    partner = a * 2 + other
    gain = gain_ref[...]
    key_gain = key_gain_ref[...]
    LEFT, RIGHT, ACROSS = 0, 1, 2

    def reach(way):
        return (me - 2, me + 2, partner)[way]

    def has(way):
        return a > 0 if way == LEFT else a < n_a - 1

    def kv_copy(which, g, block, way):
        return pltpu.make_async_remote_copy(
            src_ref=kv.at[which, g, block], dst_ref=kv.at[which, g, block],
            send_sem=kv_send.at[which, g, block, way], recv_sem=kv_recv.at[which, g, block],
            device_id=(reach(way), uly), device_id_type=MESH,
        )

    def send_on(which, g, block, way):
        @pl.when(has(way))
        def _():
            kv_copy(which, g, block, way).start()

    def gather_stage(s, g):
        if s == 0:
            for which in range(2):
                kv_copy(which, g, me, ACROSS).start()
                send_on(which, g, me, LEFT)
                send_on(which, g, me, RIGHT)
            return
        if s == 1:
            kv_copy(1, g, partner, ACROSS).wait_recv()
            send_on(1, g, partner, LEFT)
            send_on(1, g, partner, RIGHT)
        for way, shift in ((RIGHT, -1), (LEFT, 1)):
            far = a + shift * s
            near = a + shift * (s - 1)

            @pl.when((far >= 0) & (far < n_a))
            def _():
                for which in range(2):
                    kv_copy(which, g, far * 2 + b, way).wait_recv()
                    if which == 0:
                        kv_copy(which, g, far * 2 + b, ACROSS).start()
                    send_on(which, g, far * 2 + b, way)

            if s > 1:
                @pl.when((near >= 0) & (near < n_a))
                def _():
                    kv_copy(1, g, near * 2 + other, way).wait_recv()
                    if s < n_a:
                        send_on(1, g, near * 2 + other, way)

    def gathered(g):
        gather_stage(n_a, g)
        for i in range(n_a):
            kv_copy(0, g, i * 2 + other, ACROSS).wait_recv()

    def y_copy(g):
        return pltpu.make_async_remote_copy(
            src_ref=y_out.at[g], dst_ref=y_in.at[g],
            send_sem=y_send.at[g], recv_sem=y_recv.at[g],
            device_id=(partner, uly), device_id_type=MESH,
        )

    def v_copy(g):
        return pltpu.make_async_remote_copy(
            src_ref=v_out.at[g], dst_ref=v_in.at[g],
            send_sem=v_send.at[g], recv_sem=v_recv.at[g],
            device_id=(partner, uly), device_id_type=MESH,
        )

    def line_copy(kind, g, way, d):
        return pltpu.make_async_remote_copy(
            src_ref=line_out.at[kind, g, way, d - 1], dst_ref=line_in.at[kind, g, way, d - 1],
            send_sem=line_send.at[kind, g, way, d - 1], recv_sem=line_recv.at[kind, g, way, d - 1],
            device_id=(reach(way), uly), device_id_type=MESH,
        )

    def part_of(kind, i):
        return (0 if kind == 0 else 1), i * 2 + (other if kind == 2 else b)

    def line_stage(kind, g, d):
        for way, shift in ((RIGHT, 1), (LEFT, -1)):
            to = a + shift * d

            @pl.when((to >= 0) & (to < n_a))
            def _():
                half, block = part_of(kind, to)
                at = pl.ds(half * rows, rows)
                if d < n_a - 1:
                    @pl.when(has(1 - way))
                    def _():
                        line_copy(kind, g, way, d + 1).wait_recv()
                        acc[g, block, at, :] += decode(line_in, (kind, g, way, d), rows)
                encode(line_out, (kind, g, way, d - 1), acc[g, block, at, :], rows)
                line_copy(kind, g, way, d).start()

    def line_end(kind, g):
        half, block = part_of(kind, a)
        at = pl.ds(half * rows, rows)
        for way in (RIGHT, LEFT):
            @pl.when(has(1 - way))
            def _():
                line_copy(kind, g, way, 1).wait_recv()
                acc[g, block, at, :] += decode(line_in, (kind, g, way, 0), rows)
        return acc[g, block, at, :]

    def return_stage(k, g):
        if k == 1:
            for i in range(n_a):
                encode(y_out, (g, i), acc[g, i * 2 + other, 0:rows, :], rows)
            y_copy(g).start()
        if k <= n_a - 1:
            line_stage(2, g, n_a - k)
            line_stage(1, g, n_a - k)
        if k == 2:
            y_copy(g).wait_recv()
            for i in range(n_a):
                acc[g, i * 2 + b, 0:rows, :] += decode(y_in, (g, i), rows)
        if 2 <= k <= n_a:
            line_stage(0, g, n_a - k + 1)
        if k == n_a:
            encode(v_out, (g,), line_end(2, g), rows)
            v_copy(g).start()
            line_end(1, g)
        if k == n_a + 1:
            cols = pl.ds(pl.multiple_of(g * HEAD_DIM, HEAD_DIM), HEAD_DIM)
            keys = line_end(0, g) * SCALE
            unit, inverse = unit_of(key_ref[:, cols].astype(jnp.float32))
            terms[1:2, :] += jnp.sum(keys * unit, axis=0, keepdims=True)
            dk_ref[:, cols] = norm_back(keys, unit, inverse, key_gain)
            v_copy(g).wait_recv()
            values = acc[g, me, rows : 2 * rows, :] + decode(v_in, (g,), rows)
            dv_ref[:, cols] = values.astype(jnp.bfloat16)

    @pl.when(now == 0)
    def _():
        barrier = pltpu.get_barrier_semaphore()
        for d in range(1, n_blk):
            pl.semaphore_signal(
                barrier, inc=1, device_id=(lax.rem(me + d, n_blk), uly), device_id_type=MESH
            )
        for d in range(1, n_uly):
            pl.semaphore_signal(
                barrier, inc=1, device_id=(me, lax.rem(uly + d, n_uly)), device_id_type=MESH
            )
        terms[...] = jnp.zeros_like(terms)
        for g in range(KV_HEADS):
            cols = slice(g * HEAD_DIM, (g + 1) * HEAD_DIM)
            unit, _ = unit_of(key_ref[:, cols].astype(jnp.float32))
            kv[0, g, me] = (unit * key_gain).astype(jnp.bfloat16)
            kv[1, g, me] = value_ref[:, cols]
        pl.semaphore_wait(barrier, n_blk + n_uly - 2)

    def attend():
        lane = lax.broadcasted_iota(jnp.int32, (rows, HEAD_DIM), 1)
        inner = jnp.zeros((rows, HEAD_DIM), jnp.float32)
        for h in range(GROUP):
            cols = slice(h * HEAD_DIM, (h + 1) * HEAD_DIM)
            unit, _ = unit_of(q_ref[:, cols].astype(jnp.float32))
            qs[h // 2, pl.ds((h % 2) * rows, rows), :] = (unit * gain).astype(jnp.bfloat16)
            grad = do_ref[:, cols]
            dos[h // 2, pl.ds((h % 2) * rows, rows), :] = grad
            one = jnp.sum(
                grad.astype(jnp.float32) * ao_ref[:, cols].astype(jnp.float32), axis=1, keepdims=True
            )
            inner = jnp.where(lane == h, one, inner)
        inner = inner.T
        for h in range(GROUP):
            half = pl.ds((h % 2) * rows, rows)
            stats[h // 2, 0:1, half] = inner[h : h + 1, :]
            stats[h // 2, 1:2, half] = lt_ref[0, h : h + 1, :] * LOG2E

        gathered(step)
        slot = step
        for i in range(n_blk):
            kt[:, i * rows : (i + 1) * rows] = (
                kv[0, step, i].astype(jnp.float32).T.astype(jnp.bfloat16)
            )

        def one_pair(pair):
            query = qs[pair]
            grad = dos[pair]
            row_inner = stats[pair, 0:1, :]
            totals = stats[pair, 1:2, :]
            dq_t = jnp.zeros((HEAD_DIM, 2 * rows), jnp.float32)
            for c in range(n_a):
                both = pl.ds(2 * c, 2)
                part = pl.ds(c * 2 * rows, 2 * rows)
                keys = kv[0, step, both].reshape(2 * rows, HEAD_DIM)
                values = kv[1, step, both].reshape(2 * rows, HEAD_DIM)
                bias = bias_ref[part, :]
                scores = dot(keys, query, NT)
                probs = jnp.exp2(
                    scores * (SCALE * LOG2E) - totals + jnp.concatenate([bias, bias], axis=1)
                )
                dprobs = dot(values, grad, NT)
                dscores = (probs * (dprobs - row_inner)).astype(jnp.bfloat16)
                value_part = dot(probs.astype(jnp.bfloat16), grad, NN).reshape(2, rows, HEAD_DIM)
                key_part = dot(dscores, query, NN).reshape(2, rows, HEAD_DIM)
                if pair > 0:
                    value_part += acc[slot, both, rows : 2 * rows, :]
                    key_part += acc[slot, both, 0:rows, :]
                acc[slot, both, rows : 2 * rows, :] = value_part
                acc[slot, both, 0:rows, :] = key_part
                dq_t += dot(kt[:, part], dscores, NN)
            dq = dq_t.T * SCALE
            for h in range(2):
                cols = pl.ds((2 * pair + h) * HEAD_DIM, HEAD_DIM)
                one = dq[h * rows : (h + 1) * rows, :]
                unit, inverse = unit_of(q_ref[:, cols].astype(jnp.float32))
                terms[0:1, :] += jnp.sum(one * unit, axis=0, keepdims=True)
                dq_ref[:, cols] = norm_back(one, unit, inverse, gain)

        for pair in range(PAIRS):
            one_pair(pair)

    for s in range(n_a):
        @pl.when((now - s >= 0) & (now - s <= last))
        def _():
            gather_stage(s, now - s)

    @pl.when((step >= 0) & (step <= last))
    def _():
        attend()

    for k in range(1, n_a + 2):
        @pl.when((step - k + 1 >= 0) & (step - k + 1 <= last))
        def _():
            return_stage(k, step - k + 1)

    @pl.when(step == last + n_a)
    def _():
        def term_copy(ref, index, sends, recvs, d, to):
            return pltpu.make_async_remote_copy(
                src_ref=ref.at[index], dst_ref=ref.at[index],
                send_sem=sends.at[d - 1], recv_sem=recvs.at[index],
                device_id=to, device_id_type=MESH,
            )

        def share(ref, mine, count, sends, recvs, to):
            for d in range(1, count):
                term_copy(ref, mine, sends, recvs, d, to(d)).start()
            for d in range(1, count):
                term_copy(ref, lax.rem(mine + d, count), sends, recvs, d, to(d)).wait_recv()
            total = ref[0]
            for i in range(1, count):
                total = total + ref[i]
            return total

        blk_terms[me] = terms[...]
        uly_terms[uly] = share(
            blk_terms, me, n_blk, t_send, t_recv, lambda d: (lax.rem(me + d, n_blk), uly)
        )
        total = share(
            uly_terms, uly, n_uly, u_send, u_recv, lambda d: (me, lax.rem(uly + d, n_uly))
        )
        q_term_ref[...] = total[0:1, :]
        k_term_ref[...] = total[1:2, :]
        for d in range(1, n_blk):
            term_copy(blk_terms, me, t_send, t_recv, d, (lax.rem(me + d, n_blk), uly)).wait_send()
        for d in range(1, n_uly):
            term_copy(uly_terms, uly, u_send, u_recv, d, (me, lax.rem(uly + d, n_uly))).wait_send()

        def when_started(condition, copy):
            @pl.when(condition)
            def _():
                copy.wait_send()

        def drain(g, carry):
            for which in range(2):
                kv_copy(which, g, me, ACROSS).wait_send()
                for way, shift in ((RIGHT, -1), (LEFT, 1)):
                    when_started(has(way), kv_copy(which, g, me, way))
                    if which == 1:
                        when_started(has(way), kv_copy(1, g, partner, way))
                    for d in range(1, n_a):
                        far = a + shift * d
                        inside = (far >= 0) & (far < n_a)
                        on = inside & has(way)
                        when_started(on, kv_copy(which, g, far * 2 + b, way))
                        if which == 0:
                            when_started(inside, kv_copy(0, g, far * 2 + b, ACROSS))
                        else:
                            when_started(on, kv_copy(1, g, far * 2 + other, way))
            y_copy(g).wait_send()
            v_copy(g).wait_send()
            for kind in range(3):
                for d in range(1, n_a):
                    when_started(a + d < n_a, line_copy(kind, g, RIGHT, d))
                    when_started(a - d >= 0, line_copy(kind, g, LEFT, d))
            return carry

        lax.fori_loop(0, KV_HEADS, drain, 0)


def fused(q, do, ao, keys, values, lt, bias, gain, key_gain, n_blk, n_uly, rows):
    wide = GROUP * HEAD_DIM
    total = n_blk * rows
    n_a = n_blk // 2
    dma = pltpu.SemaphoreType.DMA
    head = lambda i: jnp.clip(i - n_a, 0, KV_HEADS - 1)
    side = pl.BlockSpec((rows, wide), lambda i: (0, head(i)))
    whole = pl.BlockSpec((rows, KV_HEADS * HEAD_DIM), lambda g: (0, 0))
    line = pl.BlockSpec((1, HEAD_DIM), lambda g: (0, 0))
    code = (CODE_ROWS, HEAD_DIM)
    return pl.pallas_call(
        functools.partial(fused_kernel, n_blk, n_uly, rows),
        grid=(KV_HEADS + 2 * n_a,),
        in_specs=[
            side, side, side, whole, whole,
            pl.BlockSpec((1, GROUP, rows), lambda i: (head(i), 0, 0)),
            pl.BlockSpec((total, rows), lambda g: (0, 0)),
            line, line,
        ],
        out_specs=[side, whole, whole, line, line],
        out_shape=[
            jax.ShapeDtypeStruct((rows, HEADS * HEAD_DIM), jnp.bfloat16),
            jax.ShapeDtypeStruct((rows, KV_HEADS * HEAD_DIM), jnp.bfloat16),
            jax.ShapeDtypeStruct((rows, KV_HEADS * HEAD_DIM), jnp.bfloat16),
            jax.ShapeDtypeStruct((1, HEAD_DIM), jnp.float32),
            jax.ShapeDtypeStruct((1, HEAD_DIM), jnp.float32),
        ],
        scratch_shapes=[
            pltpu.VMEM((PAIRS, 2 * rows, HEAD_DIM), jnp.bfloat16),
            pltpu.VMEM((PAIRS, 2 * rows, HEAD_DIM), jnp.bfloat16),
            pltpu.VMEM((PAIRS, 2, 2 * rows), jnp.float32),
            pltpu.VMEM((HEAD_DIM, total), jnp.bfloat16),
            pltpu.VMEM((2, KV_HEADS, n_blk, rows, HEAD_DIM), jnp.bfloat16),
            pltpu.VMEM((KV_HEADS, n_blk, 2 * rows, HEAD_DIM), jnp.float32),
            pltpu.VMEM((KV_HEADS, n_a, *code), jnp.int16),
            pltpu.VMEM((KV_HEADS, n_a, *code), jnp.int16),
            pltpu.VMEM((3, KV_HEADS, 2, n_a - 1, *code), jnp.int16),
            pltpu.VMEM((3, KV_HEADS, 2, n_a - 1, *code), jnp.int16),
            pltpu.VMEM((KV_HEADS, *code), jnp.int16),
            pltpu.VMEM((KV_HEADS, *code), jnp.int16),
            pltpu.VMEM((8, HEAD_DIM), jnp.float32),
            pltpu.VMEM((n_blk, 8, HEAD_DIM), jnp.float32),
            pltpu.VMEM((n_uly, 8, HEAD_DIM), jnp.float32),
            dma((2, KV_HEADS, n_blk, 3)),
            dma((2, KV_HEADS, n_blk)),
            dma((KV_HEADS,)),
            dma((KV_HEADS,)),
            dma((3, KV_HEADS, 2, n_a - 1)),
            dma((3, KV_HEADS, 2, n_a - 1)),
            dma((KV_HEADS,)),
            dma((KV_HEADS,)),
            dma((n_blk - 1,)),
            dma((n_blk,)),
            dma((n_uly - 1,)),
            dma((n_uly,)),
        ],
        compiler_params=pltpu.CompilerParams(
            dimension_semantics=("arbitrary",),
            vmem_limit_bytes=60 * 1024 * 1024,
            collective_id=0,
            has_side_effects=True,
        ),
        cost_estimate=pl.CostEstimate(
            flops=10 * HEADS * rows * total * HEAD_DIM,
            bytes_accessed=8 * rows * HEADS * HEAD_DIM,
            transcendentals=HEADS * rows * total,
        ),
    )(q, do, ao, keys, values, lt, bias, gain, key_gain)


def per_device(
    queries,
    key_states,
    value_states,
    attention_out,
    output_grad,
    log_totals,
    block_order,
    query_gain,
    key_gain,
):
    n_blk = lax.axis_size("blk")
    n_uly = lax.axis_size("uly")
    rows = queries.shape[1]
    me = lax.axis_index("blk")
    inside = jnp.arange(rows, dtype=jnp.int32)
    places = (block_order[:, None] * rows + inside[None, :]).reshape(-1)
    own = jnp.sum(jnp.where(jnp.arange(n_blk) == me, block_order, 0)) * rows + inside
    bias = jnp.where(places[:, None] <= own[None, :], 0.0, -jnp.inf).astype(jnp.float32)
    dq, dk, dv, query_term, key_term = fused(
        queries[0], output_grad[0], attention_out[0], key_states[0], value_states[0],
        log_totals[0].reshape(KV_HEADS, GROUP, rows), bias, query_gain[None, :],
        key_gain[None, :], n_blk, n_uly, rows,
    )
    return (dq[None], dk[None], dv[None], query_term[0], key_term[0])


def solution(mesh):
    return jax.shard_map(
        per_device,
        mesh=mesh,
        in_specs=(
            P("uly", "blk", None),
            P("uly", "blk", None),
            P("uly", "blk", None),
            P("uly", "blk", None),
            P("uly", "blk", None),
            P("uly", None, "blk"),
            P(),
            P(),
            P(),
        ),
        out_specs=(P("uly", "blk", None), P("uly", "blk", None), P("uly", "blk", None), P(), P()),
        check_vma=False,
    )
```

time: 159 us -> 129 us (0.81)
  Pallas kernels: 148 us -> 117 us
    pallas_call x1, Pallas kernels: 148 us -> 117 us  [fused(): pl.pallas_call(functools.partial(fused_kernel, n_blk, n_uly, rows), grid=...]
where the time goes in v3:
time: 129 us; the launch traced here: 128 us
  Pallas kernels  117 us (91%)
  local copies, waits for them, and re-layouts  7.37 us (6%)
  other arithmetic  2.36 us (2%)
  between operations  1.34 us (1%)
    pallas_call x1, Pallas kernels, fused(): pl.pallas_call(functools.partial(fused_kernel, n_blk, n_uly, rows), grid=...  117 us
    unnamed x13, local copies, waits for them, and re-layouts  5.96 us

profile of v3, /device:TPU:0, one launch (start us, length us, event | category | flops | bytes accessed | tf_op | source)
XLA Modules:
  0.0 128.4 jit_solution(13245711593146223067)
XLA Ops:
  0.6 1.3 %broadcast_multiply_fusion = (s32[8]{0:T(128)S(1)}, s32[]{:T(128)}) fusion(s32[8]{0:T(128)} %param.15, s32[]{:T(128)S(6)} %axis_index.15), kind=kLoop, calls=%fused_computation.5 | loop fusion | flops 31 | bytes 72 | tf_op jit(solution)/shard_map/mul | solution.py:463
  2.6 0.1 add_bitcast_fusion
  2.7 1.4 %reshape_squeeze.3.lt_ref = f32[8,10,128]{2,1,0:T(8,128)} reshape(f32[1,80,128]{2,1,0:T(8,128)} %param.14) | data formatting | bytes 81920 | tf_op jit(solution)/shard_map/reshape;squeeze | solution.py:468
  4.1 1.0 compare_select_fusion.bias_ref
  5.1 117.3 %shard_map.128 = (bf16[128,10240]{1,0:T(8,128)(2,1)}, bf16[128,1024]{1,0:T(8,128)(2,1)}, bf16[128,1024]{1,0:T(8,128)(2,1)}, f32[1,128]{1,0:T(1,128)}, f32[1,128]{1,0:T(1,128)}) custom-call(bf16[128,10240]{1,0:T(8,128)(2,1)} %bitcast.17, bf16[128,10240]{1,0:T(8,128)(2,1)} %bitcast.18, bf16[128,10240]{1,0:T(8,128)(2,1)} %bitcast.19, ...), custom_call_target="tpu_custom_call" | custom-call | flops 13421772800 | bytes 10485760 | tf_op jit(solution)/shard_map/pallas_call | solution.py:387
  122.4 0.0 copy-start.1
  122.4 0.0 copy-start
  122.4 0.0 copy-start.3
  122.4 0.0 copy-start.2
  122.4 3.5 %copy.19 = bf16[1,128,10240]{2,1,0:T(8,128)(2,1)} copy(bf16[1,128,10240]{2,1,0:T(8,128)(2,1)} %bitcast.14) | data formatting | bytes 5242880
  125.9 0.0 copy-done.1
  125.9 0.7 copy.20
  126.6 0.0 copy-done
  126.6 0.7 copy.21
  127.3 0.0 copy-done.3
  127.3 0.5 copy.22
  127.8 0.0 copy-done.2
  127.8 0.5 copy.23
  (1 shorter events, 0.0 us)
Async XLA Ops:
  122.4 3.6 %copy-start.1 = (bf16[128,1024]{1,0:T(8,128)(2,1)S(1)}, bf16[128,1024]{1,0:T(8,128)(2,1)}, u32[]{:S(2)}) copy-start(bf16[128,1024]{1,0:T(8,128)(2,1)} %get-tuple-element.11) | copy-start | bytes 786436
  122.4 4.3 %copy-start = (bf16[128,1024]{1,0:T(8,128)(2,1)S(1)}, bf16[128,1024]{1,0:T(8,128)(2,1)}, u32[]{:S(2)}) copy-start(bf16[128,1024]{1,0:T(8,128)(2,1)} %get-tuple-element.12) | copy-start | bytes 786436
  122.4 4.9 %copy-start.3 = (f32[1,128]{1,0:T(1,128)S(1)}, f32[1,128]{1,0:T(1,128)}, u32[]{:S(2)}) copy-start(f32[1,128]{1,0:T(1,128)} %get-tuple-element.13) | copy-start | bytes 1540
  122.4 5.5 %copy-start.2 = (f32[1,128]{1,0:T(1,128)S(1)}, f32[1,128]{1,0:T(1,128)}, u32[]{:S(2)}) copy-start(f32[1,128]{1,0:T(1,128)} %get-tuple-element.14) | copy-start | bytes 1540
